TPU v7x, 256 devices: a whole 4x4x8 slice. The times are simulated.
256 devices in a mesh: node: 32 (over x, z), local: 8 (over y, core).
Axes of the slice: x: 4, y: 4, z: 8, core: 2. Of those that a mesh axis runs over, the one named last changes fastest.
Arguments:
- hidden_in: bfloat16 [16384, 2048], P(('node', 'local')), may hold values from -6 to 6
- queries: bfloat16 [16384, 2048], P('node', 'local'), may hold values from -6 to 6
- key_vectors: bfloat16 [16384, 2048], P('node', 'local'), may hold values from -6 to 6
- values: bfloat16 [16384, 4096], P('node', 'local'), may hold values from -6 to 6
- out_gate: bfloat16 [16384, 4096], P('node', 'local'), may hold values from -6 to 6
- log_decay: float32 [16384, 32], P('node', 'local'), may hold values from -1 to 0
- write_rate: float32 [16384, 32], P('node', 'local'), may hold values from 0 to 1
- norm_gain: float32 [128], replicated, may hold values from 0.5 to 1.5
- out_weight: bfloat16 [4096, 2048], P('local'), may hold values from -0.09375 to 0.09375
- post_gain: float32 [2048], replicated, may hold values from 0.5 to 1.5
- expert_index: int32 [16384, 10], P('node'), may hold values from 0 to 255, all different within a row; in each aligned block of 512 rows (0 to 511, 512 to 1023, ...) at most 24 rows name the same one
- route_weight: float32 [16384, 10], P('node'), may hold values from 0.05 to 0.5
- expert_gate_up: bfloat16 [256, 2048, 1024], P(('node', 'local')), may hold values from -0.125 to 0.125
- expert_down: bfloat16 [256, 512, 2048], P(('node', 'local')), may hold values from -0.25 to 0.25
Outputs:
- layer_out: bfloat16 [16384, 2048], P(('node', 'local'))
Inputs may be any that keep to these rules, and one draw needn't show every extreme that they name: `expert_index`: each row names 10 different experts; within each aligned block of 512 rows no expert is named by more than 24 rows.
All inputs are finite; a program needn't handle non-finite values.
Results may differ from a plain program's by a relative error of at most 0.018.
Values may be sent and summed in bfloat16 or wider, within the bound.
No kernel may reach another device: no remote copies, remote signals or barrier semaphores. Data moves between devices by JAX's collectives and lax.ppermute only.
A program may use at most 128 MiB of HBM per device.

v0:
```python
import jax
import jax.numpy as jnp
from jax import lax
from jax.sharding import PartitionSpec as P

VALUE_HEADS = 32
HK = 16
DK = 128
DV = 128
TOP = 10
BLOCK = 64
EXP_DEV = 1


exact_precision = lax.Precision.HIGHEST


def carried_in(shard, axis, combine, identity):
    devices, place = (lax.axis_size(axis), lax.axis_index(axis))
    everything = jax.tree.map(
        lambda part, kind: lax.all_gather(part.astype(kind), axis),
        shard,
        (jnp.bfloat16, jnp.bfloat16),
    )
    start = jax.tree.map(
        lambda part, zero: jnp.broadcast_to(jnp.asarray(zero, part.dtype), part.shape),
        shard,
        identity,
    )

    def lap(k, before):
        reached = k < place
        new = combine(
            before, jax.tree.map(lambda part, own: part[k].astype(own.dtype), everything, shard)
        )
        return jax.tree.map(lambda a, b: jnp.where(reached, a, b), new, before)

    return lax.fori_loop(0, devices, lap, start)


def unit_rows(matrix):
    return matrix * lax.rsqrt(jnp.sum(matrix * matrix, axis=-1, keepdims=True) + 1e-06)


def rms_normalize(matrix, gain_vector):
    return (
        matrix * lax.rsqrt(jnp.mean(matrix * matrix, axis=-1, keepdims=True) + 1e-06) * gain_vector
    )


def invert_unit_lower(lower_part):
    width_rows = lower_part.shape[-1]
    identity_matrix = jnp.eye(width_rows, dtype=jnp.float32)
    powered = -lower_part
    inverse = identity_matrix + powered
    for doubling in range(width_rows.bit_length() - 2):
        powered = jnp.einsum("...ij,...jk->...ik", powered, powered, precision=exact_precision)
        inverse = jnp.einsum(
            "...ij,...jk->...ik", inverse, identity_matrix + powered, precision=exact_precision
        )
    return inverse


def block_terms(query_unit, key_unit, value_rows, cumulative, strength):
    width_rows = cumulative.shape[-1]
    positions = jnp.arange(width_rows)
    strict = positions[:, None] > positions[None, :]
    inclusive = positions[:, None] >= positions[None, :]
    spread = cumulative[..., :, None] - cumulative[..., None, :]
    decay_strict = jnp.where(strict, jnp.exp(jnp.where(strict, spread, 0.0)), 0.0)
    decay_inclusive = jnp.where(inclusive, jnp.exp(jnp.where(inclusive, spread, 0.0)), 0.0)
    key_inner = jnp.einsum("...td,...sd->...ts", key_unit, key_unit, precision=exact_precision)
    inverse = invert_unit_lower(strength[..., :, None] * decay_strict * key_inner)
    weight_values = jnp.einsum(
        "...ts,...sv->...tv", inverse, strength[..., None] * value_rows, precision=exact_precision
    )
    weight_keys = jnp.einsum(
        "...ts,...sk->...tk",
        inverse,
        (strength * jnp.exp(cumulative))[..., None] * key_unit,
        precision=exact_precision,
    )
    attention = decay_inclusive * jnp.einsum(
        "...td,...sd->...ts", query_unit, key_unit, precision=exact_precision
    )
    emitter = jnp.exp(cumulative)[..., None] * query_unit - jnp.einsum(
        "...ts,...sk->...tk", attention, weight_keys, precision=exact_precision
    )
    tail_keys = jnp.exp(cumulative[..., -1:] - cumulative)[..., None] * key_unit
    identity_matrix = jnp.eye(key_unit.shape[-1], dtype=jnp.float32)
    transition = jnp.exp(cumulative[..., -1])[..., None, None] * identity_matrix - jnp.einsum(
        "...tk,...tj->...kj", weight_keys, tail_keys, precision=exact_precision
    )
    injection = jnp.einsum(
        "...tv,...tj->...vj", weight_values, tail_keys, precision=exact_precision
    )
    return (attention, weight_values, emitter, transition, injection)


def to_blocks(matrix, blocks, heads_dev):
    return matrix.reshape(blocks, BLOCK, heads_dev, -1).transpose(0, 2, 1, 3)


def local(
    hidden_in,
    queries,
    key_vectors,
    values,
    out_gate,
    log_decay,
    write_rate,
    norm_gain,
    out_weight,
    post_gain,
    expert_index,
    route_weight,
    expert_gate_up,
    expert_down,
):
    node_count = lax.axis_size("node")
    local_count = lax.axis_size("local")
    local_index = lax.axis_index("local")
    tokens_node = queries.shape[0]
    key_heads = queries.shape[1] // DK
    heads_dev = values.shape[1] // DV
    blocks = tokens_node // BLOCK
    share_rows = tokens_node // local_count
    model_width = hidden_in.shape[1]
    capacity = 6 * tokens_node * TOP // (5 * EXP_DEV * node_count * local_count)
    groups = node_count * EXP_DEV
    flat_index = expert_index.reshape(-1)
    owner = flat_index // EXP_DEV
    local_pair = owner % local_count == local_index
    target = owner // local_count * EXP_DEV + flat_index % EXP_DEV
    member = jnp.logical_and(
        target[:, None] == jnp.arange(groups)[None, :], local_pair[:, None]
    ).astype(jnp.int32)
    before = jnp.cumsum(member, axis=0) - member
    ranking = jnp.sum(before * member, axis=1)
    slot_of_pair = jnp.where(local_pair, target * capacity + ranking, groups * capacity)
    pair_token = jnp.arange(flat_index.shape[0], dtype=jnp.int32) // TOP
    slot_token = (
        jnp.full((groups * capacity,), tokens_node, jnp.int32)
        .at[slot_of_pair]
        .set(pair_token, mode="drop")
    )
    slot_weight = (
        jnp.zeros((groups * capacity,), jnp.float32)
        .at[slot_of_pair]
        .set(route_weight.reshape(-1), mode="drop")
    )
    query_unit = unit_rows(
        queries.astype(jnp.float32).reshape(tokens_node, key_heads, DK)
    ) * DK ** (-0.5)
    query_unit = to_blocks(jnp.repeat(query_unit, VALUE_HEADS // HK, axis=1), blocks, heads_dev)
    key_unit = unit_rows(key_vectors.astype(jnp.float32).reshape(tokens_node, key_heads, DK))
    key_unit = to_blocks(jnp.repeat(key_unit, VALUE_HEADS // HK, axis=1), blocks, heads_dev)
    value_rows = to_blocks(values.astype(jnp.float32), blocks, heads_dev)
    cumulative = jnp.cumsum(log_decay.reshape(blocks, BLOCK, heads_dev), axis=1).transpose(0, 2, 1)
    strength = write_rate.reshape(blocks, BLOCK, heads_dev).transpose(0, 2, 1)
    attention, weight_values, emitter, transition, injection = block_terms(
        query_unit, key_unit, value_rows, cumulative, strength
    )
    identity_stack = jnp.broadcast_to(jnp.eye(DK, dtype=jnp.float32), (heads_dev, DK, DK))
    empty_state = jnp.zeros((heads_dev, DV, DK), jnp.float32)

    def carry_local(carried, block_maps):
        state_now, product = carried
        move_map, inject_map = block_maps
        state_next = (
            jnp.einsum("hvk,hkj->hvj", state_now, move_map, precision=exact_precision) + inject_map
        )
        product_next = jnp.einsum("hkl,hlj->hkj", product, move_map, precision=exact_precision)
        return ((state_next, product_next), (state_now, product))

    (shard_inject, shard_move), (state_starts, product_starts) = lax.scan(
        carry_local, (empty_state, identity_stack), (transition, injection)
    )
    local_core = jnp.einsum("chtk,chvk->chtv", emitter, state_starts, precision=exact_precision)
    local_core = local_core + jnp.einsum(
        "chts,chsv->chtv", attention, weight_values, precision=exact_precision
    )

    def compose(earlier, later_map):
        return (
            jnp.einsum("hkl,hlj->hkj", earlier[0], later_map[0], precision=exact_precision),
            jnp.einsum("hvl,hlj->hvj", earlier[1], later_map[0], precision=exact_precision)
            + later_map[1],
        )

    prefix_move, incoming = carried_in(
        (shard_move, shard_inject), "node", compose, (identity_stack, empty_state)
    )
    carried_starts = jnp.einsum(
        "hvk,chkj->chvj", incoming, product_starts, precision=exact_precision
    )
    core_out = local_core + jnp.einsum(
        "chtk,chvk->chtv", emitter, carried_starts, precision=exact_precision
    )
    core_out = core_out.transpose(0, 2, 1, 3).reshape(tokens_node, heads_dev, DV)
    gate_rows = out_gate.astype(jnp.float32).reshape(tokens_node, heads_dev, DV)
    gated = (
        (rms_normalize(core_out, norm_gain) * jax.nn.silu(gate_rows))
        .reshape(tokens_node, heads_dev * DV)
        .astype(jnp.bfloat16)
    )
    partial_value = jnp.dot(gated, out_weight, preferred_element_type=jnp.float32)
    mixer = lax.psum(
        lax.optimization_barrier(partial_value.astype(jnp.bfloat16))
        .astype(jnp.float32)
        .astype(jnp.bfloat16),
        "local",
    ).astype(jnp.float32)
    residual_all = lax.all_gather(hidden_in, "local", axis=0, tiled=True)
    hidden_all = residual_all.astype(jnp.float32) + mixer
    normed_all = rms_normalize(hidden_all, post_gain).astype(jnp.bfloat16)
    hidden_state = lax.dynamic_slice_in_dim(hidden_all, local_index * share_rows, share_rows, 0)
    padded_rows = jnp.concatenate([normed_all, jnp.zeros((1, model_width), jnp.bfloat16)], axis=0)
    outgoing_rows = padded_rows[slot_token].reshape(node_count, EXP_DEV, capacity, model_width)
    gate_up = jnp.einsum(
        "nesd,edf->nesf",
        lax.all_to_all(outgoing_rows, "node", split_axis=0, concat_axis=0, tiled=True),
        expert_gate_up,
        preferred_element_type=jnp.float32,
    )
    half_width = gate_up.shape[-1] // 2
    hidden_rows = (jax.nn.silu(gate_up[..., :half_width]) * gate_up[..., half_width:]).astype(
        jnp.bfloat16
    )
    results = jnp.einsum(
        "nesf,efd->nesd", hidden_rows, expert_down, preferred_element_type=jnp.float32
    ).astype(jnp.bfloat16)
    returned = lax.all_to_all(results, "node", split_axis=0, concat_axis=0, tiled=True).reshape(
        groups * capacity, model_width
    )
    contribution = (
        jnp.zeros((tokens_node, model_width), jnp.float32)
        .at[slot_token]
        .add(slot_weight[:, None] * returned.astype(jnp.float32), mode="drop")
    )
    part_moe = lax.optimization_barrier(contribution.astype(jnp.bfloat16)).astype(jnp.float32)
    moe_rows = lax.psum_scatter(
        part_moe.astype(jnp.bfloat16), "local", scatter_dimension=0, tiled=True
    ).astype(jnp.float32)
    return (hidden_state + moe_rows).astype(jnp.bfloat16)


def solution(mesh):
    return jax.shard_map(
        local,
        mesh=mesh,
        in_specs=(
            P(("node", "local"), None),
            P("node", "local"),
            P("node", "local"),
            P("node", "local"),
            P("node", "local"),
            P("node", "local"),
            P("node", "local"),
            P(),
            P("local", None),
            P(),
            P("node", None),
            P("node", None),
            P(("node", "local"), None, None),
            P(("node", "local"), None, None),
        ),
        out_specs=P(("node", "local"), None),
        check_vma=False,
    )
```

profile of v0, /device:TPU:2, one launch (start us, length us, event | category | flops | bytes accessed | tf_op | source)
XLA Modules:
  0.0 660.1 jit_solution(2403132942022185917)
XLA Ops:
  10.8 6.3 fusion.111
  39.8 2.7 fusion.116
  45.6 4.8 fusion.68
  50.4 5.3 multiply_subtract_fusion
  55.7 32.8 %while.31 = (s32[]{:T(128)}, f32[4,128,128]{1,2,0:T(8,128)S(1)}, f32[4,128,128]{1,2,0:T(8,128)S(1)}, f32[8,4,128,128]{2,3,1,0:T(8,128)}, f32[8,4,128,128]{2,3,1,...) while((s32[]{:T(128)}, f32[4,128,128]{1,2,0:T(8,128)S(1)}, ...), condition=%wide.region_4.5_spmd.clone, body=%wide.region_3.4_spmd.clone.sunk | while | flops 201523200 | bytes 3933815 | solution.py:176
  95.7 16.5 %reduce-window.6 = s32[32,40,128]{2,1,0:T(8,128)S(1)} reduce-window(s32[32,40,128]{2,1,0:T(8,128)} %fusion.81, s32[]{:T(128)} %constant.124.clone.1), window={size=1x1x128 pad=0_0x0_0x127_0}, to_apply=%region_9.10 | reduce-window | flops 20807680 | bytes 1310724 | tf_op jit(solution)/shard_map/reduce-window
  126.0 46.8 %all-gather.8.cloned.1.call-done = bf16[128,128,128]{2,1,0:T(8,128)(2,1)} async-done(((bf16[4,128,128]{2,1,0:T(8,128)(2,1)}), bf16[128,128,128]{2,1,0:T(8,128)(2,1)}) %all-gather.8.cloned.1.call-update) | async-done | bytes 4194320 | tf_op jit(solution)/shard_map/all_gather | solution.py:21
  172.9 81.6 %all-gather.10.cloned.1.call-done = bf16[128,128,128]{2,1,0:T(8,128)(2,1)} async-done(((bf16[4,128,128]{2,1,0:T(8,128)(2,1)}), bf16[128,128,128]{2,1,0:T(8,128)(2,1)}) %all-gather.10.cloned.1.call-update) | async-done | bytes 4194320 | tf_op jit(solution)/shard_map/all_gather | solution.py:21
  254.5 75.6 %while.32 = (s32[]{:T(128)}, f32[4,128,128]{1,2,0:T(8,128)S(1)}, s32[]{:T(128)}, bf16[32,4,128,128]{3,2,1,0:T(8,128)(2,1)}, bf16[32,4,128,128]{3,2,1,0:T(8,128)(2,1)}, /*index=5*/s32[]{:T(128)}, s32[]{:T(128)}) while((s32[]{:T(128)}, f32[4,128,128]{1,2,0:T(8,128)S(1)}, s32[]{:T(128)}, bf16[32,4,128,128]{3,2,1,0:T(8,128)(2,1)}, ...), condition=%wide.region_6.7_spmd.clone, body=%wide.region_5.6_spmd.clone.sunk | while | flops 100990976 | bytes 2099307 | solution.py:38
  330.1 3.6 fusion.90
  337.9 2.7 convolution_convert_fusion.1
  341.5 19.4 %scatter_custom_fusion = s32[768]{0:T(1024)S(1)} fusion(s32[5120]{0:T(1024)S(1)} %bitcast.218, s32[5120]{0:T(1024)} %add_select_fusion, s32[]{:T(128)} %constant.131.clone.1), kind=kCustom, calls=%fused_computation.176 | custom fusion | bytes 3584 | tf_op jit(solution)/shard_map/scatter | solution.py:145
  361.0 49.0 %all-reduce.3.cloned.1.call-done = bf16[512,2048]{1,0:T(8,128)(2,1)} async-done(((bf16[512,2048]{1,0:T(8,128)(2,1)}), bf16[512,2048]{1,0:T(8,128)(2,1)}) %all-reduce.3.cloned.1.call-update) | async-done | bytes 2097168 | tf_op jit(solution)/shard_map/psum | solution.py:208
  410.1 5.0 convert_add_fusion
  417.8 9.0 %gather_fusion = bf16[768,2048]{1,0:T(8,128)(2,1)} fusion(bf16[513,2048]{1,0:T(8,128)(2,1)} %concatenate.3, s32[1024]{0:T(1024)S(1)} %pad_clamp_fusion), kind=kCustom, calls=%fused_computation | custom fusion | bytes 6294528 | tf_op jit(solution)/shard_map/gather | solution.py:219
  426.8 80.0 %all_to_all.10 = bf16[32,1,24,2048]{3,2,1,0:T(8,128)(2,1)S(1)} all-to-all(bf16[32,1,24,2048]{3,2,1,0:T(8,128)(2,1)} %bitcast.201), channel_id=1, replica_groups=mesh['node'=32,'local'=8] {'node'}, dimensions={0} | all-to-all | bytes 6291456 | tf_op jit(solution)/shard_map/all_to_all | solution.py:222
  506.8 3.4 fusion.30
  510.2 3.6 fusion.25
  513.9 7.8 %all-to-all-start.1 = ((bf16[32,1,24,2048]{3,2,1,0:T(8,128)(2,1)}), bf16[32,1,24,2048]{3,2,1,0:T(8,128)(2,1)}, u32[]{:S(2)}, u32[]{:S(2)}) async-start(bf16[32,1,24,2048]{3,2,1,0:T(8,128)(2,1)} %fusion.25), calls=%async_computation.1 | async-start | bytes 6291456 | tf_op jit(solution)/shard_map/all_to_all | solution.py:233
  522.0 19.4 %scatter_custom_fusion.1 = f32[768]{0:T(1024)S(1)} fusion(s32[5120]{0:T(1024)S(1)} %bitcast.219, f32[5120]{0:T(1024)S(1)} %reshape.341, f32[]{:T(128)} %constant.121.clone.1), kind=kCustom, calls=%fused_computation.174 | custom fusion | bytes 3076 | tf_op jit(solution)/shard_map/scatter | solution.py:150
  541.4 49.9 %all-to-all-done.1 = bf16[32,1,24,2048]{3,2,1,0:T(8,128)(2,1)} async-done(((bf16[32,1,24,2048]{3,2,1,0:T(8,128)(2,1)}), bf16[32,1,24,2048]{3,2,1,0:T(8,128)(2,1)}, u32[]{:S(2)}, u32[]{:S(2)}) %all-to-all-start.1) | async-done | bytes 3145760 | tf_op jit(solution)/shard_map/all_to_all | solution.py:233
  591.3 17.1 %scatter_custom_fusion.2 = f32[512,2048]{1,0:T(8,128)} fusion(s32[768]{0:T(1024)S(1)} %get-tuple-element.282, bf16[768,2048]{1,0:T(8,128)(2,1)} %bitcast.51, f32[768]{0:T(1024)S(1)} %scatter_custom_fusion.1, f32[]{:T(128)} %constant.121.clone.1), kind=kCustom, calls=%fused_computation.31 | custom fusion | flops 4718592 | bytes 7344132 | tf_op jit(solution)/shard_map/scatter-add | solution.py:239
  608.5 3.9 convert_element_type.127
  612.4 39.1 %reduce-scatter.2.cloned.1.call-done = bf16[64,2048]{1,0:T(8,128)(2,1)} async-done(((bf16[512,2048]{1,0:T(8,128)(2,1)}), bf16[64,2048]{1,0:T(8,128)(2,1)}) %reduce-scatter.2.cloned.1.call-update) | async-done | bytes 262160 | tf_op jit(solution)/shard_map/reduce_scatter | solution.py:242
  (327 shorter events, 166.9 us)
Async XLA Ops:
  6.5 503.7 %copy-start = (bf16[1,512,2048]{2,1,0:T(8,128)(2,1)S(1)}, bf16[1,512,2048]{2,1,0:T(8,128)(2,1)}, u32[]{:S(2)}) copy-start(bf16[1,512,2048]{2,1,0:T(8,128)(2,1)} %param.31) | copy-start | bytes 6291460
  6.5 166.3 %all-gather.8.cloned.1.call-start = ((), (), s32[]{:S(2)}) async-start(), calls=%async_computation.6 | async-start | bytes 4325376 | tf_op jit(solution)/shard_map/all_gather | solution.py:21
  7.2 3.3 copy-start.27
  20.8 21.7 %copy-start.1 = (f32[512,2,2,128]{3,0,2,1:T(8,128)}, f32[512,2,2,128]{3,0,2,1:T(8,128)S(1)}, u32[]{:S(2)}) copy-start(f32[512,2,2,128]{3,0,2,1:T(8,128)S(1)} %broadcast_in_dim.90) | copy-start | bytes 3145732
  34.0 3.4 copy-start.28
  37.4 5.1 copy-start.19
  37.4 5.1 copy-start.20
  44.3 6.0 copy-start.3
  45.6 4.8 copy-start.5
  50.4 5.3 copy-start.15
  55.7 35.3 %copy-start.23 = (s32[512,10]{0,1:T(8,128)S(1)}, s32[512,10]{0,1:T(8,128)}, u32[]{:S(2)}) copy-start(s32[512,10]{0,1:T(8,128)} %param.28) | copy-start | bytes 61444
  89.3 165.2 %all-gather.10.cloned.1.call-start = ((), (), s32[]{:S(2)}) async-start(), calls=%async_computation.7 | async-start | bytes 4325376 | tf_op jit(solution)/shard_map/all_gather | solution.py:21
  90.1 270.9 %all-gather.6.cloned.1.call-start = ((), (), s32[]{:S(2)}) async-start(), calls=%async_computation.3 | async-start | bytes 2359296 | tf_op jit(solution)/shard_map/all_gather | solution.py:214
  90.9 319.2 %all-reduce.3.cloned.1.call-start = ((), (), s32[]{:S(2)}) async-start(), calls=%async_computation.4 | async-start | bytes 4194304 | tf_op jit(solution)/shard_map/psum | solution.py:208
  114.3 2.7 copy-start.21
  330.1 3.7 copy-start.8
  330.1 3.7 copy-start.12
  361.0 54.1 %copy-start.26 = (f32[2048]{0:T(1024)S(1)}, f32[2048]{0:T(1024)}, u32[]{:S(2)}) copy-start(f32[2048]{0:T(1024)} %param.27) | copy-start | bytes 24580
  410.1 5.0 copy-start.9
  410.1 5.0 copy-start.10
  426.8 80.0 %copy-start.30 = (bf16[1,2048,1024]{2,1,0:T(8,128)(2,1)S(1)}, bf16[1,2048,1024]{2,1,0:T(8,128)(2,1)}, u32[]{:S(2)}) copy-start(bf16[1,2048,1024]{2,1,0:T(8,128)(2,1)} %param.30) | copy-start | bytes 12582916
  513.9 7.8 %copy-start.24 = (f32[512,10]{0,1:T(8,128)S(1)}, f32[512,10]{0,1:T(8,128)}, u32[]{:S(2)}) copy-start(f32[512,10]{0,1:T(8,128)} %param.29) | copy-start | bytes 61444
  513.9 77.5 %all-to-all-start.1 = ((bf16[32,1,24,2048]{3,2,1,0:T(8,128)(2,1)}), bf16[32,1,24,2048]{3,2,1,0:T(8,128)(2,1)}, u32[]{:S(2)}, u32[]{:S(2)}) async-start(bf16[32,1,24,2048]{3,2,1,0:T(8,128)(2,1)} %fusion.25), calls=%async_computation.1 | async-start | bytes 6291456 | tf_op jit(solution)/shard_map/all_to_all | solution.py:233
  521.6 129.9 %reduce-scatter.2.cloned.1.call-start = ((), (), s32[]{:S(2)}) async-start(), calls=%async_computation.5 | async-start | bytes 2359296 | tf_op jit(solution)/shard_map/reduce_scatter | solution.py:242
  (15 other events, 25.7 us)
Sparse Core Ops, SparseCore 0:
  89.4 83.3 all-gather.7
  175.5 78.9 all-gather.9
  256.4 26.2 all-gather.5
  340.8 69.2 all-reduce.2
  612.5 38.9 reduce-scatter.1
where the time goes:
time: 673 us; the launch traced here: 660 us
  waiting for transfers between devices  267 us (40%)
  matrix products  119 us (18%)
  local copies, waits for them, and re-layouts  101 us (15%)
  blocking collectives  80 us (12%)
  other arithmetic  68.8 us (10%)
  between operations  14 us (2%)
  starting transfers between devices  7.92 us (1%)
    all_gather x2, waiting for transfers between devices, carried_in(): lax.all_gather(part.astype(kind), axis)  128 us
    all_to_all x1, blocking collectives, local(): lax.all_to_all(outgoing_rows, 'node', split_axis=0, concat_axis=0, tiled=...  80 us
    all_to_all x1, waiting for transfers between devices, local(): lax.all_to_all(results, 'node', split_axis=0, concat_axis=0, tiled=True)  49.9 us
    psum x1, waiting for transfers between devices, local(): lax.psum(lax.optimization_barrier(partial_value.astype(jnp.bfloat16)).ast...  49 us
    dot_general x32, matrix products, compose(): jnp.einsum('hvl,hlj->hvj', earlier[1], later_map[0], precision=exact_prec...  39.6 us
    reduce_scatter x1, waiting for transfers between devices, local(): lax.psum_scatter(part_moe.astype(jnp.bfloat16), 'local', scatter_dimensio...  39.1 us
    dynamic_slice x64, local copies, waits for them, and re-layouts, lap(): part[k].astype(own.dtype)  33.7 us
    scatter x1, local copies, waits for them, and re-layouts, local(): slot_token = jnp.full((groups * capacity,), tokens_node, jnp.int32).at[sl...  19.4 us
  transfers between devices with their start and end apart: 6, of which 5 were waited for; matrix products, arithmetic and copies ran while one was open for 24% of the time, Pallas kernels for 0%

commit v1 on v0

v1 whole, which is shorter than its diff:
```python
import jax
import jax.numpy as jnp
from jax import lax
from jax.experimental import pallas as pl
from jax.experimental.pallas import tpu as pltpu
from jax.sharding import PartitionSpec as P

DK = 128
DV = 128
HEADS = 4
BLOCK = 64
STACK = HEADS * BLOCK
SPLIT = 8
LOCAL = 8

f32 = jnp.float32
bf16 = jnp.bfloat16


def mm(a, b):
    return jnp.dot(a.astype(bf16), b.astype(bf16), preferred_element_type=f32)


def mm_t(a, b):
    return lax.dot_general(
        a.astype(bf16), b.astype(bf16), (((1,), (1,)), ((), ())), preferred_element_type=f32
    )


def t_mm(a, b):
    return lax.dot_general(
        a.astype(bf16), b.astype(bf16), (((0,), (0,)), ((), ())), preferred_element_type=f32
    )


def stack_rows(pieces):
    return jnp.concatenate(pieces, axis=0)


def head_column(columns):
    return stack_rows([columns[:, h : h + 1] for h in range(HEADS)])


def unit_scale(rows):
    wide = rows.astype(f32)
    return lax.rsqrt(jnp.sum(wide * wide, axis=-1, keepdims=True) + 1e-06)


def stacked_keys(key_ref, rows):
    keys = key_ref[rows, :]
    pair = [keys[:, :DK], keys[:, DK:]]
    scales = [unit_scale(p) for p in pair]
    return (
        stack_rows([pair[0], pair[0], pair[1], pair[1]]),
        stack_rows([scales[0], scales[0], scales[1], scales[1]]),
    )


def grid_places():
    row = lax.broadcasted_iota(jnp.int32, (STACK, STACK), 0)
    col = lax.broadcasted_iota(jnp.int32, (STACK, STACK), 1)
    return row, col, (row // BLOCK) == (col // BLOCK)


def as_row(column, row, col):
    return jnp.sum(jnp.where(row == col, column, 0.0), axis=0, keepdims=True)


def maps_kernel(
    key_ref, value_ref, decay_ref, rate_ref,
    payload_ref, cum_ref, inner_ref, values_ref, starts_ref,
    rate_s, tail_s, state_s,
):
    tokens = key_ref.shape[0]
    blocks = tokens // BLOCK
    lane = lax.broadcasted_iota(jnp.int32, (HEADS, tokens), 1) % BLOCK
    total = decay_ref[...]
    step = 1
    while step < BLOCK:
        total = total + jnp.where(lane >= step, pltpu.roll(total, step, 1), 0.0)
        step *= 2
    cum_ref[...] = total.T
    rate_s[...] = rate_ref[...].T

    def one_block(b):
        rows = pl.ds(b * BLOCK, BLOCK)
        row, col, same = grid_places()
        keys, scale = stacked_keys(key_ref, rows)
        cum = cum_ref[rows, :]
        cum_col = head_column(cum)
        rate_col = head_column(rate_s[rows, :])
        last_col = stack_rows(
            [jnp.broadcast_to(cum[BLOCK - 1 : BLOCK, h : h + 1], (BLOCK, 1)) for h in range(HEADS)]
        )
        strict = jnp.logical_and(same, row > col)
        spread = jnp.where(strict, cum_col - as_row(cum_col, row, col), 0.0)
        power = jnp.where(
            strict,
            -(jnp.exp(spread) * mm_t(keys, keys)) * ((rate_col * scale) * as_row(scale, row, col)),
            0.0,
        )
        raw = value_ref[rows, :]
        wide = keys.astype(f32)
        answer = jnp.concatenate(
            [
                rate_col * stack_rows([raw[:, h * DV : (h + 1) * DV] for h in range(HEADS)]).astype(f32),
                (rate_col * jnp.exp(cum_col) * scale) * wide,
            ],
            axis=1,
        )
        reach = 1
        while reach < BLOCK:
            answer = answer + mm(power, answer)
            reach *= 2
            if reach < BLOCK:
                power = mm(power, power)
        values_ref[b] = answer[:, :DV]
        inner_ref[b] = answer[:, DV:].astype(bf16)
        tail_s[b] = ((jnp.exp(last_col - cum_col) * scale) * wide).astype(bf16)

    def two_blocks(i, carry):
        one_block(2 * i)
        one_block(2 * i + 1)
        return carry

    lax.fori_loop(0, blocks // 2, two_blocks, 0)

    place = lax.broadcasted_iota(jnp.int32, (DK, DV + DK), 0)
    lane_place = lax.broadcasted_iota(jnp.int32, (DK, DV + DK), 1)
    for h in range(HEADS):
        state_s[h] = jnp.where(lane_place == place + DV, 1.0, 0.0)

    def advance(b, carry):
        last = cum_ref[pl.ds(b * BLOCK + BLOCK - 1, 1), :]
        for h in range(HEADS):
            part = slice(h * BLOCK, (h + 1) * BLOCK)
            state = state_s[h]
            rounded = state.astype(bf16)
            starts_ref[b, h] = rounded
            change = mm(inner_ref[b, part, :], rounded)
            given = jnp.concatenate([values_ref[b, part, :] - change[:, :DV], -change[:, DV:]], axis=1)
            state_s[h] = jnp.exp(last[:, h : h + 1]) * state + t_mm(tail_s[b, part, :], given)
        return carry

    lax.fori_loop(0, blocks, advance, 0)
    share = DV // SPLIT
    for h in range(HEADS):
        state = state_s[h]
        inject = state[:, :DV].T.astype(bf16)
        move = state[:, DV:].T.astype(bf16)
        for s in range(SPLIT):
            payload_ref[h * SPLIT + s, :DK, :] = move
            payload_ref[h * SPLIT + s, DK:, :] = inject[s * share : (s + 1) * share, :]


def shard_maps(keys, values, decay, rate):
    tokens = keys.shape[0]
    blocks = tokens // BLOCK
    return pl.pallas_call(
        maps_kernel,
        out_shape=(
            jax.ShapeDtypeStruct((HEADS * SPLIT, DK + DV // SPLIT, DK), bf16),
            jax.ShapeDtypeStruct((tokens, HEADS), f32),
            jax.ShapeDtypeStruct((blocks, STACK, DK), bf16),
            jax.ShapeDtypeStruct((blocks, STACK, DV), f32),
            jax.ShapeDtypeStruct((blocks, HEADS, DK, DV + DK), bf16),
        ),
        scratch_shapes=[
            pltpu.VMEM((tokens, HEADS), f32),
            pltpu.VMEM((blocks, STACK, DK), bf16),
            pltpu.VMEM((HEADS, DK, DV + DK), f32),
        ],
        compiler_params=pltpu.CompilerParams(vmem_limit_bytes=48 * 2**20),
        name="shard_maps",
    )(keys, values, decay, rate)


def reads_kernel(query_ref, key_ref, cum_ref, inner_ref, values_ref, starts_ref, core_ref, reach_ref):
    blocks = query_ref.shape[0] // BLOCK

    def one_block(b):
        rows = pl.ds(b * BLOCK, BLOCK)
        row, col, same = grid_places()
        keys, scale = stacked_keys(key_ref, rows)
        queries, query_scale = stacked_keys(query_ref, rows)
        query_scale = query_scale * DK ** (-0.5)
        cum_col = head_column(cum_ref[rows, :])
        inclusive = jnp.logical_and(same, row >= col)
        spread = jnp.where(inclusive, cum_col - as_row(cum_col, row, col), 0.0)
        attention = jnp.where(
            inclusive,
            jnp.exp(spread) * mm_t(queries, keys) * (query_scale * as_row(scale, row, col)),
            0.0,
        )
        both = mm(attention, jnp.concatenate([values_ref[b].astype(bf16), inner_ref[b]], axis=1))
        emitter = ((jnp.exp(cum_col) * query_scale) * queries.astype(f32) - both[:, DV:]).astype(bf16)
        for h in range(HEADS):
            part = slice(h * BLOCK, (h + 1) * BLOCK)
            read = mm(emitter[part, :], starts_ref[b, h])
            core_ref[rows, h * DV : (h + 1) * DV] = both[part, :DV] + read[:, :DV]
            reach_ref[rows, h * DK : (h + 1) * DK] = read[:, DV:].astype(bf16)

    def two_blocks(i, carry):
        one_block(2 * i)
        one_block(2 * i + 1)
        return carry

    lax.fori_loop(0, blocks // 2, two_blocks, 0)


def block_reads(queries, keys, cum, inner, values, starts):
    tokens = keys.shape[0]
    return pl.pallas_call(
        reads_kernel,
        out_shape=(
            jax.ShapeDtypeStruct((tokens, HEADS * DV), f32),
            jax.ShapeDtypeStruct((tokens, HEADS * DK), bf16),
        ),
        compiler_params=pltpu.CompilerParams(vmem_limit_bytes=48 * 2**20),
        cost_estimate=pl.CostEstimate(flops=2 * 10**9, bytes_accessed=8 * 10**6, transcendentals=10**6),
        name="block_reads",
    )(queries, keys, cum, inner, values, starts)


def chain_kernel(maps_ref, start_ref):
    share = start_ref.shape[1]
    state = jnp.zeros((share, DK), f32)
    for k in range(maps_ref.shape[0]):
        high = state.astype(bf16)
        start_ref[k] = high
        low = (state - high.astype(f32)).astype(bf16)
        moved = jnp.dot(
            jnp.concatenate([high, low], axis=0), maps_ref[k, :DK, :], preferred_element_type=f32
        )
        state = moved[:share] + moved[share:] + maps_ref[k, DK:, :].astype(f32)


def chain(maps):
    return pl.pallas_call(
        chain_kernel,
        out_shape=jax.ShapeDtypeStruct((maps.shape[0], maps.shape[1] - DK, DK), bf16),
        compiler_params=pltpu.CompilerParams(vmem_limit_bytes=32 * 2**20),
        name="state_chain",
    )(maps)


def gated_kernel(core_side, core_ref, reach_ref, start_ref, gate_ref, gain_ref, own_ref, other_ref):
    tokens = core_ref.shape[0]
    share = tokens // LOCAL
    side = core_side[0]
    for chip in range(LOCAL // 2):
        for ref, parity in ((own_ref, side), (other_ref, 1 - side)):
            rows = pl.ds((2 * chip + parity) * share, share)
            for h in range(HEADS):
                lanes = slice(h * DV, (h + 1) * DV)
                core = core_ref[rows, lanes] + mm_t(reach_ref[rows, lanes], start_ref[lanes, :])
                core = core * lax.rsqrt(jnp.mean(core * core, axis=-1, keepdims=True) + 1e-06)
                gate = gate_ref[rows, lanes].astype(f32)
                ref[chip * share : (chip + 1) * share, lanes] = (
                    core * gain_ref[...] * (gate / (1.0 + jnp.exp(-gate)))
                ).astype(bf16)


def gated_halves(side, core, reach, starts, gate, gain):
    tokens = core.shape[0]
    vmem = pl.BlockSpec(memory_space=pltpu.VMEM)
    half = jax.ShapeDtypeStruct((tokens // 2, HEADS * DV), bf16)
    return pl.pallas_call(
        gated_kernel,
        out_shape=(half, half),
        in_specs=[pl.BlockSpec(memory_space=pltpu.SMEM)] + [vmem] * 5,
        out_specs=(vmem, vmem),
        compiler_params=pltpu.CompilerParams(vmem_limit_bytes=32 * 2**20),
        name="gated_halves",
    )(side, core, reach, starts, gate, gain)


def project_kernel(own_ref, other_ref, own_weight, other_weight, out_ref):
    out_ref[...] = (mm(own_ref[...], own_weight[...]) + mm(other_ref[...], other_weight[...])).astype(bf16)


def project(own, other, own_weight, other_weight):
    rows, depth = own.shape
    width = own_weight.shape[1]
    tile = 512
    rows_spec = pl.BlockSpec((rows, depth), lambda i: (0, 0))
    weight_spec = pl.BlockSpec((depth, tile), lambda i: (0, i))
    return pl.pallas_call(
        project_kernel,
        out_shape=jax.ShapeDtypeStruct((rows, width), bf16),
        grid=(width // tile,),
        in_specs=[rows_spec, rows_spec, weight_spec, weight_spec],
        out_specs=pl.BlockSpec((rows, tile), lambda i: (0, i)),
        compiler_params=pltpu.CompilerParams(vmem_limit_bytes=32 * 2**20),
        name="project",
    )(own, other, own_weight, other_weight)


def residual_kernel(parts_ref, hidden_ref, gain_ref, state_ref, normed_ref):
    state = hidden_ref[...].astype(f32)
    for part in range(parts_ref.shape[0]):
        state = state + parts_ref[part].astype(f32)
    state_ref[...] = state
    normed = state * lax.rsqrt(jnp.mean(state * state, axis=-1, keepdims=True) + 1e-06) * gain_ref[...]
    for copy in range(normed_ref.shape[0]):
        normed_ref[copy] = normed.astype(bf16)


def residual(parts, hidden, gain):
    return pl.pallas_call(
        residual_kernel,
        out_shape=(
            jax.ShapeDtypeStruct(hidden.shape, f32),
            jax.ShapeDtypeStruct(parts.shape, bf16),
        ),
        compiler_params=pltpu.CompilerParams(vmem_limit_bytes=32 * 2**20),
        name="residual",
    )(parts, hidden, gain)


def routing_kernel(capacity, place_ref, index_ref, weight_ref, pick_ref, merge_ref, slot_s, share_s, wide_s):
    top, tokens = index_ref.shape
    groups = slot_s.shape[0]
    ids = lax.broadcasted_iota(jnp.int32, (groups, 1), 0) * LOCAL + place_ref[0]
    member = jnp.zeros((groups, tokens), f32)
    share = jnp.zeros((groups, tokens), f32)
    for j in range(top):
        hit = index_ref[j : j + 1, :] == ids
        member = jnp.where(hit, 1.0, member)
        share = jnp.where(hit, weight_ref[j : j + 1, :], share)
    earlier = lax.broadcasted_iota(jnp.int32, (tokens, tokens), 0) < lax.broadcasted_iota(
        jnp.int32, (tokens, tokens), 1
    )
    rank = mm(member, jnp.where(earlier, 1.0, 0.0))
    slot_s[...] = jnp.where(member > 0.0, rank, -1.0)
    share_s[...] = share
    several = 4
    span = several * capacity
    for i in range(groups // several):
        slot = slot_s[i * several : (i + 1) * several, :]
        part = share_s[i * several : (i + 1) * several, :]
        place = lax.broadcasted_iota(jnp.int32, (several, capacity, tokens), 1).astype(f32)
        hit = slot[:, None, :] == place
        pick_ref[i * span : (i + 1) * span, :] = (
            jnp.where(hit, 1.0, 0.0).reshape(span, tokens).astype(bf16)
        )
        wide_s[i * span : (i + 1) * span, :] = jnp.where(hit, part[:, None, :], 0.0).reshape(
            span, tokens
        )
    for i in range(groups * capacity // 128):
        merge_ref[:, i * 128 : (i + 1) * 128] = wide_s[i * 128 : (i + 1) * 128, :].T.astype(bf16)


def routing(place, index, weight, groups, capacity):
    top, tokens = index.shape
    slots = groups * capacity
    vmem = pl.BlockSpec(memory_space=pltpu.VMEM)
    return pl.pallas_call(
        lambda *refs: routing_kernel(capacity, *refs),
        out_shape=(
            jax.ShapeDtypeStruct((slots, tokens), bf16),
            jax.ShapeDtypeStruct((tokens, slots), bf16),
        ),
        in_specs=[pl.BlockSpec(memory_space=pltpu.SMEM), vmem, vmem],
        out_specs=(vmem, vmem),
        scratch_shapes=[
            pltpu.VMEM((groups, tokens), f32),
            pltpu.VMEM((groups, tokens), f32),
            pltpu.VMEM((slots, tokens), f32),
        ],
        compiler_params=pltpu.CompilerParams(vmem_limit_bytes=32 * 2**20),
        cost_estimate=pl.CostEstimate(flops=3 * 10**9, bytes_accessed=6 * 10**6, transcendentals=0),
        name="routing",
    )(place, index, weight)


def pick_kernel(pick_ref, own_ref, other_ref, out_ref):
    half = own_ref.shape[0]
    out_ref[...] = (mm(pick_ref[:, :half], own_ref[...]) + mm(pick_ref[:, half:], other_ref[...])).astype(bf16)


def pick_rows(pick, own, other):
    slots, tokens = pick.shape
    half, width = own.shape
    tile = 512
    half_spec = pl.BlockSpec((half, tile), lambda i: (0, i))
    return pl.pallas_call(
        pick_kernel,
        out_shape=jax.ShapeDtypeStruct((slots, width), bf16),
        grid=(width // tile,),
        in_specs=[pl.BlockSpec((slots, tokens), lambda i: (0, 0)), half_spec, half_spec],
        out_specs=pl.BlockSpec((slots, tile), lambda i: (0, i)),
        compiler_params=pltpu.CompilerParams(vmem_limit_bytes=32 * 2**20),
        name="pick_rows",
    )(pick, own, other)


def merge_kernel(merge_ref, rows_ref, out_ref):
    out_ref[...] = mm(merge_ref[...], rows_ref[...]).astype(bf16)


def merge_add_kernel(merge_ref, rows_ref, add_ref, out_ref):
    out_ref[...] = (mm(merge_ref[...], rows_ref[...]) + add_ref[...].astype(f32)).astype(bf16)


def merge_rows(merge, half, rows, *add):
    tokens, slots = merge.shape
    width = rows.shape[1]
    tile = 512
    out_spec = pl.BlockSpec((tokens // 2, tile), lambda i: (0, i))
    return pl.pallas_call(
        merge_add_kernel if add else merge_kernel,
        out_shape=jax.ShapeDtypeStruct((tokens // 2, width), bf16),
        grid=(width // tile,),
        in_specs=[
            pl.BlockSpec((tokens // 2, slots), lambda i: (half, 0)),
            pl.BlockSpec((slots, tile), lambda i: (0, i)),
        ]
        + [out_spec] * len(add),
        out_specs=out_spec,
        compiler_params=pltpu.CompilerParams(vmem_limit_bytes=32 * 2**20),
        name="merge_rows",
    )(merge, rows, *add)


def swap_cores(array):
    return lax.ppermute(array, "local", [(i, i ^ 1) for i in range(LOCAL)])


def across_chips(array):
    groups = [[side + 2 * chip for chip in range(LOCAL // 2)] for side in range(2)]
    return lax.all_to_all(
        array, "local", split_axis=0, concat_axis=0, tiled=True, axis_index_groups=groups
    )


def across_nodes(array):
    return lax.all_to_all(array, "node", split_axis=0, concat_axis=0, tiled=True)


def local(
    hidden_in, queries, key_vectors, values, out_gate, log_decay, write_rate, norm_gain,
    out_weight, post_gain, expert_index, route_weight, expert_gate_up, expert_down,
):
    node_count = lax.axis_size("node")
    local_index = lax.axis_index("local")
    side = local_index % 2
    tokens, top = expert_index.shape
    chips = LOCAL // 2
    share = tokens // LOCAL
    width = hidden_in.shape[1]
    capacity = 6 * tokens * top // (5 * node_count * LOCAL)
    side_array = side.astype(jnp.int32).reshape(1)

    other_weight = swap_cores(out_weight)

    def by_side(array):
        split = array.T.reshape(top, chips, 2, share)
        split = jnp.where(side == 0, split, split[:, :, ::-1])
        return split.transpose(0, 2, 1, 3).reshape(top, tokens)

    pick, merge = routing(
        local_index.astype(jnp.int32).reshape(1), by_side(expert_index), by_side(route_weight),
        node_count, capacity,
    )

    payload, cum, inner, value_rows, starts = shard_maps(key_vectors, values, log_decay.T, write_rate.T)
    maps = across_nodes(payload)
    core, reach = block_reads(queries, key_vectors, cum, inner, value_rows, starts)
    carried = across_nodes(chain(maps)).reshape(HEADS * DV, DK)
    own_half, other_half = gated_halves(
        side_array, core, reach, carried, out_gate, norm_gain.reshape(1, DV)
    )
    partial = project(own_half, swap_cores(other_half), out_weight, other_weight)
    parts = across_chips(partial.reshape(chips, share, width))
    hidden_state, normed = residual(parts, hidden_in, post_gain.reshape(1, width))
    own_rows = across_chips(normed).reshape(chips * share, width)
    rows = pick_rows(pick, own_rows, swap_cores(own_rows)).reshape(node_count, capacity, width)
    rows = across_nodes(rows).reshape(node_count * capacity, width)
    gate_up = jnp.dot(rows, expert_gate_up[0], preferred_element_type=f32)
    half_width = gate_up.shape[1] // 2
    hidden_rows = (jax.nn.silu(gate_up[:, :half_width]) * gate_up[:, half_width:]).astype(bf16)
    results = jnp.dot(hidden_rows, expert_down[0], preferred_element_type=f32).astype(bf16)
    returned = across_nodes(results.reshape(node_count, capacity, width)).reshape(
        node_count * capacity, width
    )
    given = swap_cores(merge_rows(merge, 1, returned))
    summed = merge_rows(merge, 0, returned, given)
    arrived = across_chips(summed.reshape(chips, share, width))
    return (hidden_state + jnp.sum(arrived.astype(f32), axis=0)).astype(bf16)


def solution(mesh):
    return jax.shard_map(
        local,
        mesh=mesh,
        in_specs=(
            P(("node", "local"), None),
            P("node", "local"),
            P("node", "local"),
            P("node", "local"),
            P("node", "local"),
            P("node", "local"),
            P("node", "local"),
            P(),
            P("local", None),
            P(),
            P("node", None),
            P("node", None),
            P(("node", "local"), None, None),
            P(("node", "local"), None, None),
        ),
        out_specs=P(("node", "local"), None),
        check_vma=False,
    )
```

time: 673 us -> 332 us (0.49); the launches traced: 660 us -> 329 us
  waiting for transfers between devices: 267 us -> 34.6 us
  blocking collectives: 80 us -> 214 us
  matrix products: 119 us -> 5.26 us
  local copies, waits for them, and re-layouts: 101 us -> 17.6 us
  other arithmetic: 68.8 us -> 0.93 us
  Pallas kernels: 0 us -> 36.2 us
  between operations: 14 us -> 0.31 us
  starting transfers between devices: 7.92 us -> 19.8 us
    all_to_all x1 -> x5, blocking collectives: 80 us -> 214 us  [the longest x2 159 us: across_nodes(): lax.all_to_all(array, 'node', split_axis=0, concat_axis=0, tiled=True)]
    all_gather x3 -> x0, waiting for transfers between devices: 128 us -> none  [the longest x2 128 us: carried_in(): lax.all_gather(part.astype(kind), axis)]
    dot_general x72 -> x2, matrix products: 119 us -> 5.26 us  [the longest x1 3.42 us: local(): gate_up = jnp.dot(rows, expert_gate_up[0], preferred_element_type=f32)]
    psum x1 -> x0, waiting for transfers between devices: 49 us -> none  [local(): lax.psum(lax.optimization_barrier(partial_value.astype(jnp.bfloat16)).ast...]
    reduce_scatter x1 -> x0, waiting for transfers between devices: 39.1 us -> none  [local(): lax.psum_scatter(part_moe.astype(jnp.bfloat16), 'local', scatter_dimensio...]
    scatter x2 -> x0, local copies, waits for them, and re-layouts: 38.8 us -> none  [the longest x1 19.4 us: local(): slot_token = jnp.full((groups * capacity,), tokens_node, jnp.int32).at[sl...]
    pallas_call x0 -> x10, Pallas kernels: none -> 36.2 us  [the longest x1 15 us: shard_maps(): pl.pallas_call(maps_kernel, out_shape=(jax.ShapeDtypeStruct((HEADS * SPLI...]
    dynamic_slice x64 -> x0, local copies, waits for them, and re-layouts: 33.7 us -> none  [lap(): part[k].astype(own.dtype)]
  transfers between devices with their start and end apart: 6 -> 6, of which waited for: 5 -> 4; matrix products, arithmetic and copies ran while one was open for 24% -> 0% of each run, Pallas kernels for 0% -> 3%
where the time goes in v1:
time: 332 us; the launch traced here: 329 us
  blocking collectives  214 us (64%)
  Pallas kernels  36.2 us (11%)
  waiting for transfers between devices  34.6 us (10%)
  starting transfers between devices  19.8 us (6%)
  local copies, waits for them, and re-layouts  17.6 us (5%)
  matrix products  5.26 us (2%)
    all_to_all x2, blocking collectives, across_nodes(): lax.all_to_all(array, 'node', split_axis=0, concat_axis=0, tiled=True)  159 us
    all_to_all x3, blocking collectives, across_chips(): lax.all_to_all(array, 'local', split_axis=0, concat_axis=0, tiled=True, a...  54.7 us
    all_to_all x2, waiting for transfers between devices, across_nodes(): lax.all_to_all(array, 'node', split_axis=0, concat_axis=0, tiled=True)  28.7 us
    all_to_all x2, starting transfers between devices, across_nodes(): lax.all_to_all(array, 'node', split_axis=0, concat_axis=0, tiled=True)  19.5 us
    unnamed x56, local copies, waits for them, and re-layouts  17.2 us
    pallas_call x1, Pallas kernels, shard_maps(): pl.pallas_call(maps_kernel, out_shape=(jax.ShapeDtypeStruct((HEADS * SPLI...  15 us
  transfers between devices with their start and end apart: 6, of which 4 were waited for; matrix products, arithmetic and copies ran while one was open for 0% of the time, Pallas kernels for 3%

profile of v1, /device:TPU:2, one launch (start us, length us, event | category | flops | bytes accessed | tf_op | source)
XLA Modules:
  0.0 328.7 jit_solution(10973044842107387802)
XLA Ops:
  0.0 1.2 copy-done.3
  3.5 15.0 %shard_maps.1 = (bf16[32,144,128]{2,1,0:T(8,128)(2,1)S(1)}, f32[512,4]{1,0:T(8,128)S(1)}, bf16[8,256,128]{2,1,0:T(8,128)(2,1)S(1)}, f32[8,256,128]{2,1,0:T(8,128)S(1)}, bf16[8,4,128,256]{3,2,1,0:T(8,128)(2,1)S(1)}) custom-call(bf16[512,256]{1,0:T(8,128)(2,1)S(1)} %copy-done.9, bf16[512,512]{1,0:T(8,128)(2,1)S(1)} %copy-done.3, f32[4,512]{1,0:T(4,128)S(1)} %bitcast.35, ...), custom_call_target="tpu_custom_call" | custom-call | tf_op jit(solution)/shard_map/shard_maps/pallas_call | solution.py:159
  19.6 1.3 copy-done.16
  23.4 11.8 %all-to-all-start = ((bf16[32,144,128]{2,1,0:T(8,128)(2,1)}), bf16[32,144,128]{2,1,0:T(8,128)(2,1)S(1)}, u32[]{:S(2)}, u32[]{:S(2)}) async-start(bf16[32,144,128]{2,1,0:T(8,128)(2,1)} %copy-done.2), calls=%async_computation | async-start | bytes 2359296 | tf_op jit(solution)/shard_map/all_to_all | solution.py:438
  35.3 28.7 %all-to-all-done.maps_ref = bf16[32,144,128]{2,1,0:T(8,128)(2,1)S(1)} async-done(((bf16[32,144,128]{2,1,0:T(8,128)(2,1)}), bf16[32,144,128]{2,1,0:T(8,128)(2,1)S(1)}, u32[]{:S(2)}, u32[]{:S(2)}) %all-to-all-start) | async-done | bytes 1179680 | tf_op jit(solution)/shard_map/all_to_all | solution.py:438
  64.0 4.4 %state_chain.1 = bf16[32,16,128]{2,1,0:T(8,128)(2,1)} custom-call(bf16[32,144,128]{2,1,0:T(8,128)(2,1)S(1)} %all-to-all-done.maps_ref), custom_call_target="tpu_custom_call" | custom-call | tf_op jit(solution)/shard_map/state_chain/pallas_call | solution.py:239
  68.4 7.7 %all-to-all-start.1 = ((bf16[32,16,128]{2,1,0:T(8,128)(2,1)}), bf16[32,16,128]{2,1,0:T(8,128)(2,1)S(1)}, u32[]{:S(2)}, u32[]{:S(2)}) async-start(bf16[32,16,128]{2,1,0:T(8,128)(2,1)} %state_chain.1), calls=%async_computation.1 | async-start | bytes 262144 | tf_op jit(solution)/shard_map/all_to_all | solution.py:438
  76.2 1.6 copy-done.17
  77.8 1.2 copy-done.19
  81.9 3.8 %block_reads.1 = (f32[512,512]{1,0:T(8,128)S(1)}, bf16[512,512]{1,0:T(8,128)(2,1)S(1)}) custom-call(bf16[512,256]{1,0:T(8,128)(2,1)S(1)} %copy-done.22, bf16[512,256]{1,0:T(8,128)(2,1)S(1)} %copy-done.10, f32[512,4]{1,0:T(8,128)S(1)} %copy-done.24, bf16[8,256,128]{2,1,0:T(8,128)(2,1)S(1)} %copy-done.21, f32[8,256,128]{2,1,0:T(8,128)S(1)} %copy-done.19, ...), custom_call_target="tpu_custom_call" | custom-call | flops 2000000000 | bytes 8000000 | tf_op jit(solution)/shard_map/block_reads/pallas_call | solution.py:213
  89.9 1.5 collective-permute-done.other_ref
  91.4 3.6 %project.1 = bf16[256,2048]{1,0:T(8,128)(2,1)S(1)} custom-call(bf16[256,512]{1,0:T(8,128)(2,1)S(1)} %get-tuple-element.25.own_ref, bf16[256,512]{1,0:T(8,128)(2,1)S(1)} %collective-permute-done.other_ref, bf16[512,2048]{1,0:T(8,128)(2,1)S(1)} %copy-done.1, bf16[512,2048]{1,0:T(8,128)(2,1)} %collective-permute-done.1.other_weight), custom_call_target="tpu_custom_call" | custom-call | tf_op jit(solution)/shard_map/project/pallas_call | solution.py:288
  95.0 19.8 %all_to_all.35.parts_ref = bf16[4,64,2048]{2,1,0:T(8,128)(2,1)S(1)} all-to-all(bf16[4,64,2048]{2,1,0:T(8,128)(2,1)S(1)} %bitcast.32), channel_id=1, replica_groups={{0,2,4,6},{1,3,5,7},{8,10,12,14},{9,11,13,15},{16,18,20,22},{17,19,21,2..., dimensions={0} | all-to-all | bytes 2097152 | tf_op jit(solution)/shard_map/all_to_all | solution.py:432
  115.1 16.7 %all_to_all.36 = bf16[4,64,2048]{2,1,0:T(8,128)(2,1)S(1)} all-to-all(bf16[4,64,2048]{2,1,0:T(8,128)(2,1)S(1)} %get-tuple-element.30), channel_id=1, replica_groups={{0,2,4,6},{1,3,5,7},{8,10,12,14},{9,11,13,15},{16,18,20,22},{17,19,21,2..., dimensions={0} | all-to-all | bytes 2097152 | tf_op jit(solution)/shard_map/all_to_all | solution.py:432
  132.9 1.7 collective-permute-done.2.other_ref
  134.6 3.9 %pick_rows.1 = bf16[768,2048]{1,0:T(8,128)(2,1)S(1)} custom-call(bf16[768,512]{1,0:T(8,128)(2,1)S(1)} %get-tuple-element.29.pick_ref, bf16[256,2048]{1,0:T(8,128)(2,1)S(1)} %bitcast.31, bf16[256,2048]{1,0:T(8,128)(2,1)} %collective-permute-done.2.other_ref), custom_call_target="tpu_custom_call" | custom-call | tf_op jit(solution)/shard_map/pick_rows/pallas_call | solution.py:387
  138.5 81.2 %all_to_all.37 = bf16[32,24,2048]{2,1,0:T(8,128)(2,1)S(1)} all-to-all(bf16[32,24,2048]{2,1,0:T(8,128)(2,1)S(1)} %bitcast.29), channel_id=1, replica_groups=mesh['node'=32,'local'=8] {'node'}, dimensions={0} | all-to-all | bytes 6291456 | tf_op jit(solution)/shard_map/all_to_all | solution.py:438
  219.6 3.4 %fusion = f32[768,1024]{1,0:T(8,128)S(1)} fusion(bf16[768,2048]{1,0:T(8,128)(2,1)S(1)} %bitcast.39, bf16[1,2048,1024]{2,1,0:T(8,128)(2,1)S(1)} %copy-done.27), kind=kOutput, calls=%fused_computation | convolution fusion | flops 3221225472 | bytes 10485760 | tf_op jit(solution)/shard_map/dot_general | solution.py:480
  223.1 1.8 convolution_convert_fusion
  224.9 78.2 %all_to_all.38 = bf16[32,24,2048]{2,1,0:T(8,128)(2,1)S(1)} all-to-all(bf16[32,24,2048]{2,1,0:T(8,128)(2,1)S(1)} %bitcast.40), channel_id=1, replica_groups=mesh['node'=32,'local'=8] {'node'}, dimensions={0} | all-to-all | bytes 6291456 | tf_op jit(solution)/shard_map/all_to_all | solution.py:438
  303.1 1.8 merge_rows.2
  305.0 2.6 collective-permute-done.3.add_ref
  307.6 1.9 merge_rows.3
  309.6 18.2 %all_to_all.39 = bf16[4,64,2048]{2,1,0:T(8,128)(2,1)S(1)} all-to-all(bf16[4,64,2048]{2,1,0:T(8,128)(2,1)S(1)} %bitcast.33), channel_id=1, replica_groups={{0,2,4,6},{1,3,5,7},{8,10,12,14},{9,11,13,15},{16,18,20,22},{17,19,21,2..., dimensions={0} | all-to-all | bytes 2097152 | tf_op jit(solution)/shard_map/all_to_all | solution.py:432
  (71 shorter events, 15.4 us)
Async XLA Ops:
  0.0 223.1 %copy-start = (bf16[1,512,2048]{2,1,0:T(8,128)(2,1)S(1)}, bf16[1,512,2048]{2,1,0:T(8,128)(2,1)}, u32[]{:S(2)}) copy-start(bf16[1,512,2048]{2,1,0:T(8,128)(2,1)} %param.27) | copy-start | bytes 6291460
  0.0 1.2 copy-start.3
  18.5 1.1 copy-start.2
  19.6 1.3 copy-start.16
  23.4 52.7 %copy-start.10 = (bf16[512,256]{1,0:T(8,128)(2,1)S(1)}, bf16[512,256]{1,0:T(8,128)(2,1)}, u32[]{:S(2)}) copy-start(bf16[512,256]{1,0:T(8,128)(2,1)} %key_ref.3) | copy-start | bytes 786436
  23.4 40.6 %all-to-all-start = ((bf16[32,144,128]{2,1,0:T(8,128)(2,1)}), bf16[32,144,128]{2,1,0:T(8,128)(2,1)S(1)}, u32[]{:S(2)}, u32[]{:S(2)}) async-start(bf16[32,144,128]{2,1,0:T(8,128)(2,1)} %copy-done.2), calls=%async_computation | async-start | bytes 2359296 | tf_op jit(solution)/shard_map/all_to_all | solution.py:438
  35.2 54.7 %collective-permute-start.1 = (bf16[512,2048]{1,0:T(8,128)(2,1)}, bf16[512,2048]{1,0:T(8,128)(2,1)}, u32[]{:S(2)}, u32[]{:S(2)}) collective-permute-start(bf16[512,2048]{1,0:T(8,128)(2,1)} %own_weight.1), channel_id=1, source_target_pairs={{0,1},{1,0},{2,3},{3,2},{4,5},{5,4},{6,7},{7,6},{8,9},{9,8},{10,11... | collective-permute-start | bytes 6291464 | tf_op jit(solution)/shard_map/ppermute | solution.py:427
  68.4 18.2 %all-to-all-start.1 = ((bf16[32,16,128]{2,1,0:T(8,128)(2,1)}), bf16[32,16,128]{2,1,0:T(8,128)(2,1)S(1)}, u32[]{:S(2)}, u32[]{:S(2)}) async-start(bf16[32,16,128]{2,1,0:T(8,128)(2,1)} %state_chain.1), calls=%async_computation.1 | async-start | bytes 262144 | tf_op jit(solution)/shard_map/all_to_all | solution.py:438
  76.2 1.6 copy-start.17
  77.8 1.2 copy-start.19
  79.0 1.0 copy-start.21
  81.9 4.6 %copy-start.15 = (f32[128]{0:T(128)S(1)}, f32[128]{0:T(128)}, u32[]{:S(2)}) copy-start(f32[128]{0:T(128)} %param.21) | copy-start | bytes 1540
  86.6 4.8 %copy-start.1 = (bf16[512,2048]{1,0:T(8,128)(2,1)S(1)}, bf16[512,2048]{1,0:T(8,128)(2,1)}, u32[]{:S(2)}) copy-start(bf16[512,2048]{1,0:T(8,128)(2,1)} %own_weight.1) | copy-start | bytes 6291460
  86.6 1.2 copy-start.6
  89.8 1.6 collective-permute-start
  95.0 19.8 %copy-start.11 = (bf16[64,2048]{1,0:T(8,128)(2,1)S(1)}, bf16[64,2048]{1,0:T(8,128)(2,1)}, u32[]{:S(2)}) copy-start(bf16[64,2048]{1,0:T(8,128)(2,1)} %hidden_ref.1) | copy-start | bytes 786436
  95.0 19.8 %copy-start.14 = (f32[2048]{0:T(1024)S(1)}, f32[2048]{0:T(1024)}, u32[]{:S(2)}) copy-start(f32[2048]{0:T(1024)} %param.23) | copy-start | bytes 24580
  114.8 17.0 %copy-start.25 = (s32[512,10]{0,1:T(8,128)S(1)}, s32[512,10]{0,1:T(8,128)}, u32[]{:S(2)}) copy-start(s32[512,10]{0,1:T(8,128)} %param.24) | copy-start | bytes 61444
  114.8 17.2 %copy-start.26 = (f32[512,10]{0,1:T(8,128)S(1)}, f32[512,10]{0,1:T(8,128)}, u32[]{:S(2)}) copy-start(f32[512,10]{0,1:T(8,128)} %param.25) | copy-start | bytes 61444
  115.1 16.7 %copy-start.4 = (f32[64,2048]{1,0:T(8,128)}, f32[64,2048]{1,0:T(8,128)S(1)}, u32[]{:S(2)}) copy-start(f32[64,2048]{1,0:T(8,128)S(1)} %get-tuple-element.27) | copy-start | bytes 1572868
  131.8 2.8 collective-permute-start.2
  138.4 81.2 %copy-start.27 = (bf16[1,2048,1024]{2,1,0:T(8,128)(2,1)S(1)}, bf16[1,2048,1024]{2,1,0:T(8,128)(2,1)}, u32[]{:S(2)}) copy-start(bf16[1,2048,1024]{2,1,0:T(8,128)(2,1)} %param.26) | copy-start | bytes 12582916
  304.9 2.7 collective-permute-start.3
  309.6 18.4 %copy-start.5 = (f32[64,2048]{1,0:T(8,128)S(1)}, f32[64,2048]{1,0:T(8,128)}, u32[]{:S(2)}) copy-start(f32[64,2048]{1,0:T(8,128)} %copy-done.4) | copy-start | bytes 1572868
  (10 other events, 8.6 us)

commit v2 on v1

--- a/solution.py
+++ b/solution.py
@@ -10,7 +10,8 @@
 HEADS = 4
 BLOCK = 64
 STACK = HEADS * BLOCK
-SPLIT = 8
+SPLIT = 2
+NODE_ROW = 8
 LOCAL = 8
 
 f32 = jnp.float32
@@ -69,7 +70,7 @@
 def maps_kernel(
     key_ref, value_ref, decay_ref, rate_ref,
     payload_ref, cum_ref, inner_ref, values_ref, starts_ref,
-    rate_s, tail_s, state_s,
+    rate_s, tail_s, state_s, values_s,
 ):
     tokens = key_ref.shape[0]
     blocks = tokens // BLOCK
@@ -114,16 +115,13 @@
             reach *= 2
             if reach < BLOCK:
                 power = mm(power, power)
-        values_ref[b] = answer[:, :DV]
+        values_s[b] = answer[:, :DV]
+        values_ref[b] = answer[:, :DV].astype(bf16)
         inner_ref[b] = answer[:, DV:].astype(bf16)
         tail_s[b] = ((jnp.exp(last_col - cum_col) * scale) * wide).astype(bf16)
 
-    def two_blocks(i, carry):
-        one_block(2 * i)
-        one_block(2 * i + 1)
-        return carry
-
-    lax.fori_loop(0, blocks // 2, two_blocks, 0)
+    for b in range(blocks):
+        one_block(b)
 
     place = lax.broadcasted_iota(jnp.int32, (DK, DV + DK), 0)
     lane_place = lax.broadcasted_iota(jnp.int32, (DK, DV + DK), 1)
@@ -138,11 +136,11 @@
             rounded = state.astype(bf16)
             starts_ref[b, h] = rounded
             change = mm(inner_ref[b, part, :], rounded)
-            given = jnp.concatenate([values_ref[b, part, :] - change[:, :DV], -change[:, DV:]], axis=1)
+            given = jnp.concatenate([values_s[b, part, :] - change[:, :DV], -change[:, DV:]], axis=1)
             state_s[h] = jnp.exp(last[:, h : h + 1]) * state + t_mm(tail_s[b, part, :], given)
         return carry
 
-    lax.fori_loop(0, blocks, advance, 0)
+    lax.fori_loop(0, blocks, advance, 0, unroll=True)
     share = DV // SPLIT
     for h in range(HEADS):
         state = state_s[h]
@@ -162,15 +160,16 @@
             jax.ShapeDtypeStruct((HEADS * SPLIT, DK + DV // SPLIT, DK), bf16),
             jax.ShapeDtypeStruct((tokens, HEADS), f32),
             jax.ShapeDtypeStruct((blocks, STACK, DK), bf16),
-            jax.ShapeDtypeStruct((blocks, STACK, DV), f32),
+            jax.ShapeDtypeStruct((blocks, STACK, DV), bf16),
             jax.ShapeDtypeStruct((blocks, HEADS, DK, DV + DK), bf16),
         ),
         scratch_shapes=[
             pltpu.VMEM((tokens, HEADS), f32),
             pltpu.VMEM((blocks, STACK, DK), bf16),
             pltpu.VMEM((HEADS, DK, DV + DK), f32),
+            pltpu.VMEM((blocks, STACK, DV), f32),
         ],
-        compiler_params=pltpu.CompilerParams(vmem_limit_bytes=48 * 2**20),
+        compiler_params=pltpu.CompilerParams(vmem_limit_bytes=60 * 2**20),
         name="shard_maps",
     )(keys, values, decay, rate)
 
@@ -192,7 +191,7 @@
             jnp.exp(spread) * mm_t(queries, keys) * (query_scale * as_row(scale, row, col)),
             0.0,
         )
-        both = mm(attention, jnp.concatenate([values_ref[b].astype(bf16), inner_ref[b]], axis=1))
+        both = mm(attention, jnp.concatenate([values_ref[b], inner_ref[b]], axis=1))
         emitter = ((jnp.exp(cum_col) * query_scale) * queries.astype(f32) - both[:, DV:]).astype(bf16)
         for h in range(HEADS):
             part = slice(h * BLOCK, (h + 1) * BLOCK)
@@ -200,12 +199,8 @@
             core_ref[rows, h * DV : (h + 1) * DV] = both[part, :DV] + read[:, :DV]
             reach_ref[rows, h * DK : (h + 1) * DK] = read[:, DV:].astype(bf16)
 
-    def two_blocks(i, carry):
-        one_block(2 * i)
-        one_block(2 * i + 1)
-        return carry
-
-    lax.fori_loop(0, blocks // 2, two_blocks, 0)
+    for b in range(blocks):
+        one_block(b)
 
 
 def block_reads(queries, keys, cum, inner, values, starts):
@@ -216,32 +211,61 @@
             jax.ShapeDtypeStruct((tokens, HEADS * DV), f32),
             jax.ShapeDtypeStruct((tokens, HEADS * DK), bf16),
         ),
-        compiler_params=pltpu.CompilerParams(vmem_limit_bytes=48 * 2**20),
+        compiler_params=pltpu.CompilerParams(vmem_limit_bytes=60 * 2**20),
         cost_estimate=pl.CostEstimate(flops=2 * 10**9, bytes_accessed=8 * 10**6, transcendentals=10**6),
         name="block_reads",
     )(queries, keys, cum, inner, values, starts)
 
 
-def chain_kernel(maps_ref, start_ref):
-    share = start_ref.shape[1]
-    state = jnp.zeros((share, DK), f32)
+def step(state, move):
+    rows = state.shape[0]
+    high = state.astype(bf16)
+    low = (state - high.astype(f32)).astype(bf16)
+    moved = jnp.dot(jnp.concatenate([high, low], axis=0), move, preferred_element_type=f32)
+    return moved[:rows] + moved[rows:]
+
+
+def row_total_kernel(maps_ref, total_ref):
+    total = maps_ref[0].astype(f32)
+    for k in range(1, maps_ref.shape[0]):
+        moved = step(total, maps_ref[k, :DK, :])
+        total = jnp.concatenate([moved[:DK], moved[DK:] + maps_ref[k, DK:, :].astype(f32)], axis=0)
+    for copy in range(total_ref.shape[0]):
+        total_ref[copy] = total.astype(bf16)
+
+
+def row_total(maps, rows):
+    return pl.pallas_call(
+        row_total_kernel,
+        out_shape=jax.ShapeDtypeStruct((rows,) + maps.shape[1:], bf16),
+        compiler_params=pltpu.CompilerParams(vmem_limit_bytes=32 * 2**20),
+        name="row_total",
+    )(maps)
+
+
+def starts_kernel(row_ref, totals_ref, maps_ref, start_ref):
+    def apply(state, ref, k):
+        return step(state, ref[k, :DK, :]) + ref[k, DK:, :].astype(f32)
+
+    state = jnp.zeros(start_ref.shape[1:], f32)
+    for k in range(totals_ref.shape[0] - 1):
+        state = jnp.where(k < row_ref[0], apply(state, totals_ref, k), state)
     for k in range(maps_ref.shape[0]):
-        high = state.astype(bf16)
-        start_ref[k] = high
-        low = (state - high.astype(f32)).astype(bf16)
-        moved = jnp.dot(
-            jnp.concatenate([high, low], axis=0), maps_ref[k, :DK, :], preferred_element_type=f32
-        )
-        state = moved[:share] + moved[share:] + maps_ref[k, DK:, :].astype(f32)
-
-
-def chain(maps):
-    return pl.pallas_call(
-        chain_kernel,
+        start_ref[k] = state.astype(bf16)
+        if k + 1 < maps_ref.shape[0]:
+            state = apply(state, maps_ref, k)
+
+
+def shard_starts(row, totals, maps):
+    vmem = pl.BlockSpec(memory_space=pltpu.VMEM)
+    return pl.pallas_call(
+        starts_kernel,
         out_shape=jax.ShapeDtypeStruct((maps.shape[0], maps.shape[1] - DK, DK), bf16),
-        compiler_params=pltpu.CompilerParams(vmem_limit_bytes=32 * 2**20),
-        name="state_chain",
-    )(maps)
+        in_specs=[pl.BlockSpec(memory_space=pltpu.SMEM), vmem, vmem],
+        out_specs=vmem,
+        compiler_params=pltpu.CompilerParams(vmem_limit_bytes=32 * 2**20),
+        name="shard_starts",
+    )(row, totals, maps)
 
 
 def gated_kernel(core_side, core_ref, reach_ref, start_ref, gate_ref, gain_ref, own_ref, other_ref):
@@ -434,6 +458,22 @@
     )
 
 
+def along_row(array):
+    nodes = lax.axis_size("node")
+    groups = [[row + z for z in range(NODE_ROW)] for row in range(0, nodes, NODE_ROW)]
+    return lax.all_to_all(
+        array, "node", split_axis=0, concat_axis=0, tiled=True, axis_index_groups=groups
+    )
+
+
+def across_rows(array):
+    nodes = lax.axis_size("node")
+    groups = [[row + z for row in range(0, nodes, NODE_ROW)] for z in range(NODE_ROW)]
+    return lax.all_to_all(
+        array, "node", split_axis=0, concat_axis=0, tiled=True, axis_index_groups=groups
+    )
+
+
 def across_nodes(array):
     return lax.all_to_all(array, "node", split_axis=0, concat_axis=0, tiled=True)
 
@@ -465,9 +505,12 @@
     )
 
     payload, cum, inner, value_rows, starts = shard_maps(key_vectors, values, log_decay.T, write_rate.T)
-    maps = across_nodes(payload)
+    maps = along_row(payload)
     core, reach = block_reads(queries, key_vectors, cum, inner, value_rows, starts)
-    carried = across_nodes(chain(maps)).reshape(HEADS * DV, DK)
+    maps, core, reach, pick, merge = lax.optimization_barrier((maps, core, reach, pick, merge))
+    totals = across_rows(row_total(maps, node_count // NODE_ROW))
+    row = (lax.axis_index("node") // NODE_ROW).astype(jnp.int32).reshape(1)
+    carried = along_row(shard_starts(row, totals, maps)).reshape(HEADS * DV, DK)
     own_half, other_half = gated_halves(
         side_array, core, reach, carried, out_gate, norm_gain.reshape(1, DV)
     )

time: 332 us -> 302 us (0.910)
  waiting for transfers between devices: 34.6 us -> 17.2 us
  local copies, waits for them, and re-layouts: 17.6 us -> 6.78 us
  starting transfers between devices: 19.8 us -> 13.5 us
  blocking collectives: 214 us -> 220 us
    all_to_all x2, waiting for transfers between devices: 28.7 us -> 10.4 us  [the longest x1 5.51 us: along_row(): lax.all_to_all(array, 'node', split_axis=0, concat_axis=0, tiled=True, ax...]
    unnamed x56 -> x24, local copies, waits for them, and re-layouts: 17.2 us -> 4.89 us
    all_to_all x0 -> x1, blocking collectives: none -> 11.5 us  [along_row(): lax.all_to_all(array, 'node', split_axis=0, concat_axis=0, tiled=True, ax...]
    all_to_all x2, starting transfers between devices: 19.5 us -> 13.3 us  [the longest x1 8.48 us: along_row(): lax.all_to_all(array, 'node', split_axis=0, concat_axis=0, tiled=True, ax...]
    all_to_all x2, blocking collectives: 159 us -> 154 us  [across_nodes(): lax.all_to_all(array, 'node', split_axis=0, concat_axis=0, tiled=True)]
  transfers between devices with their start and end apart: 6 -> 6, of which waited for: 4 -> 5; matrix products, arithmetic and copies ran while one was open for 0% -> 1% of each run, Pallas kernels for 3% -> 8%
where the time goes in v2:
time: 302 us; the launch traced here: 299 us
  blocking collectives  220 us (73%)
  Pallas kernels  34.7 us (11%)
  waiting for transfers between devices  17.2 us (6%)
  starting transfers between devices  13.5 us (4%)
  local copies, waits for them, and re-layouts  6.78 us (2%)
  matrix products  5.25 us (2%)
    all_to_all x2, blocking collectives, across_nodes(): lax.all_to_all(array, 'node', split_axis=0, concat_axis=0, tiled=True)  154 us
    all_to_all x3, blocking collectives, across_chips(): lax.all_to_all(array, 'local', split_axis=0, concat_axis=0, tiled=True, a...  54.5 us
    pallas_call x1, Pallas kernels, shard_maps(): pl.pallas_call(maps_kernel, out_shape=(jax.ShapeDtypeStruct((HEADS * SPLI...  14.3 us
    all_to_all x1, blocking collectives, along_row(): lax.all_to_all(array, 'node', split_axis=0, concat_axis=0, tiled=True, ax...  11.5 us
    all_to_all x1, starting transfers between devices, along_row(): lax.all_to_all(array, 'node', split_axis=0, concat_axis=0, tiled=True, ax...  8.48 us
    ppermute x4, waiting for transfers between devices, swap_cores(): return lax.ppermute(array, 'local', [(i, i ^ 1) for i in range(LOCAL)])  6.83 us
    pallas_call x1, Pallas kernels, block_reads(): pl.pallas_call(reads_kernel, out_shape=(jax.ShapeDtypeStruct((tokens, HEA...  6.22 us
  transfers between devices with their start and end apart: 6, of which 5 were waited for; matrix products, arithmetic and copies ran while one was open for 1% of the time, Pallas kernels for 8%

profile of v2, /device:TPU:2, one launch (start us, length us, event | category | flops | bytes accessed | tf_op | source)
XLA Modules:
  0.0 299.1 jit_solution(17952816306251905893)
XLA Ops:
  0.0 14.3 %shard_maps.1 = (bf16[8,192,128]{2,1,0:T(8,128)(2,1)}, f32[512,4]{1,0:T(8,128)}, bf16[8,256,128]{2,1,0:T(8,128)(2,1)}, bf16[8,256,128]{2,1,0:T(8,128)(2,1)}, bf16[8,4,128,256]{3,2,1,0:T(8,128)(2,1)}) custom-call(bf16[512,256]{1,0:T(8,128)(2,1)} %key_ref.3, bf16[512,512]{1,0:T(8,128)(2,1)} %value_ref.1, f32[4,512]{1,0:T(4,128)} %bitcast.42, f32[4,512]{1,0:T(4,128)} %bitcast.43), custom_call_target="tpu_custom_call" | custom-call | tf_op jit(solution)/shard_map/shard_maps/pallas_call | solution.py:157
  14.3 8.5 %all-to-all-start = ((bf16[8,192,128]{2,1,0:T(8,128)(2,1)}), bf16[8,192,128]{2,1,0:T(8,128)(2,1)S(1)}, u32[]{:S(2)}, u32[]{:S(2)}) async-start(bf16[8,192,128]{2,1,0:T(8,128)(2,1)} %get-tuple-element.23), calls=%async_computation | async-start | bytes 786432 | tf_op jit(solution)/shard_map/all_to_all | solution.py:464
  24.8 6.2 %block_reads.1 = (f32[512,512]{1,0:T(8,128)}, bf16[512,512]{1,0:T(8,128)(2,1)}) custom-call(bf16[512,256]{1,0:T(8,128)(2,1)} %query_ref.1, bf16[512,256]{1,0:T(8,128)(2,1)} %key_ref.3, f32[512,4]{1,0:T(8,128)} %get-tuple-element.24.cum_ref, bf16[8,256,128]{2,1,0:T(8,128)(2,1)} %get-tuple-element.25.inner_ref, ...), custom_call_target="tpu_custom_call" | custom-call | flops 2000000000 | bytes 8000000 | tf_op jit(solution)/shard_map/block_reads/pallas_call | solution.py:208
  32.5 5.5 %all-to-all-done.maps_ref = bf16[8,192,128]{2,1,0:T(8,128)(2,1)S(1)} async-done(((bf16[8,192,128]{2,1,0:T(8,128)(2,1)}), bf16[8,192,128]{2,1,0:T(8,128)(2,1)S(1)}, u32[]{:S(2)}, u32[]{:S(2)}) %all-to-all-start) | async-done | bytes 393248 | tf_op jit(solution)/shard_map/all_to_all | solution.py:464
  38.0 1.0 row_total.1
  39.7 4.8 %all-to-all-start.1 = ((bf16[4,192,128]{2,1,0:T(8,128)(2,1)}), bf16[4,192,128]{2,1,0:T(8,128)(2,1)S(1)}, u32[]{:S(2)}, u32[]{:S(2)}) async-start(bf16[4,192,128]{2,1,0:T(8,128)(2,1)} %copy-done.3), calls=%async_computation.1 | async-start | bytes 393216 | tf_op jit(solution)/shard_map/all_to_all | solution.py:472
  44.5 4.9 %all-to-all-done.1.totals_ref = bf16[4,192,128]{2,1,0:T(8,128)(2,1)S(1)} async-done(((bf16[4,192,128]{2,1,0:T(8,128)(2,1)}), bf16[4,192,128]{2,1,0:T(8,128)(2,1)S(1)}, u32[]{:S(2)}, u32[]{:S(2)}) %all-to-all-start.1) | async-done | bytes 196640 | tf_op jit(solution)/shard_map/all_to_all | solution.py:472
  49.4 1.3 shard_starts.1
  50.7 11.5 %all_to_all.40 = bf16[8,64,128]{2,1,0:T(8,128)(2,1)S(1)} all-to-all(bf16[8,64,128]{2,1,0:T(8,128)(2,1)S(1)} %shard_starts.1), channel_id=1, replica_groups={{0,8,16,24,32,40,48,56},{64,72,80,88,96,104,112,120},{128,136,144,152,1..., dimensions={0} | all-to-all | bytes 262144 | tf_op jit(solution)/shard_map/all_to_all | solution.py:464
  62.1 1.2 copy-done.2
  66.5 1.5 collective-permute-done.other_ref
  68.1 3.6 %project.1 = bf16[256,2048]{1,0:T(8,128)(2,1)S(1)} custom-call(bf16[256,512]{1,0:T(8,128)(2,1)S(1)} %get-tuple-element.35.own_ref, bf16[256,512]{1,0:T(8,128)(2,1)S(1)} %collective-permute-done.other_ref, bf16[512,2048]{1,0:T(8,128)(2,1)S(1)} %copy-done.1, bf16[512,2048]{1,0:T(8,128)(2,1)} %collective-permute-done.1.other_weight), custom_call_target="tpu_custom_call" | custom-call | tf_op jit(solution)/shard_map/project/pallas_call | solution.py:312
  71.7 19.8 %all_to_all.41.parts_ref = bf16[4,64,2048]{2,1,0:T(8,128)(2,1)S(1)} all-to-all(bf16[4,64,2048]{2,1,0:T(8,128)(2,1)S(1)} %bitcast.33), channel_id=1, replica_groups={{0,2,4,6},{1,3,5,7},{8,10,12,14},{9,11,13,15},{16,18,20,22},{17,19,21,2..., dimensions={0} | all-to-all | bytes 2097152 | tf_op jit(solution)/shard_map/all_to_all | solution.py:456
  91.8 16.6 %all_to_all.42 = bf16[4,64,2048]{2,1,0:T(8,128)(2,1)S(1)} all-to-all(bf16[4,64,2048]{2,1,0:T(8,128)(2,1)S(1)} %get-tuple-element.40), channel_id=1, replica_groups={{0,2,4,6},{1,3,5,7},{8,10,12,14},{9,11,13,15},{16,18,20,22},{17,19,21,2..., dimensions={0} | all-to-all | bytes 2097152 | tf_op jit(solution)/shard_map/all_to_all | solution.py:456
  108.5 2.7 collective-permute-done.2.other_ref
  111.1 2.7 pick_rows.1
  113.8 76.1 %all_to_all.43 = bf16[32,24,2048]{2,1,0:T(8,128)(2,1)S(1)} all-to-all(bf16[32,24,2048]{2,1,0:T(8,128)(2,1)S(1)} %bitcast.30), channel_id=1, replica_groups=mesh['node'=32,'local'=8] {'node'}, dimensions={0} | all-to-all | bytes 6291456 | tf_op jit(solution)/shard_map/all_to_all | solution.py:478
  189.9 3.4 %fusion = f32[768,1024]{1,0:T(8,128)S(1)} fusion(bf16[768,2048]{1,0:T(8,128)(2,1)S(1)} %bitcast.38, bf16[1,2048,1024]{2,1,0:T(8,128)(2,1)S(1)} %copy-done.11), kind=kOutput, calls=%fused_computation | convolution fusion | flops 3221225472 | bytes 10485760 | tf_op jit(solution)/shard_map/dot_general | solution.py:523
  193.3 1.8 convolution_convert_fusion
  195.1 78.4 %all_to_all.44 = bf16[32,24,2048]{2,1,0:T(8,128)(2,1)S(1)} all-to-all(bf16[32,24,2048]{2,1,0:T(8,128)(2,1)S(1)} %bitcast.39), channel_id=1, replica_groups=mesh['node'=32,'local'=8] {'node'}, dimensions={0} | all-to-all | bytes 6291456 | tf_op jit(solution)/shard_map/all_to_all | solution.py:478
  273.6 1.8 merge_rows.2
  275.5 2.6 collective-permute-done.3.add_ref
  278.1 1.9 merge_rows.3
  280.0 18.1 %all_to_all.45 = bf16[4,64,2048]{2,1,0:T(8,128)(2,1)S(1)} all-to-all(bf16[4,64,2048]{2,1,0:T(8,128)(2,1)S(1)} %bitcast.34), channel_id=1, replica_groups={{0,2,4,6},{1,3,5,7},{8,10,12,14},{9,11,13,15},{16,18,20,22},{17,19,21,2..., dimensions={0} | all-to-all | bytes 2097152 | tf_op jit(solution)/shard_map/all_to_all | solution.py:456
  (41 shorter events, 8.5 us)
Async XLA Ops:
  0.0 193.3 %copy-start = (bf16[1,512,2048]{2,1,0:T(8,128)(2,1)S(1)}, bf16[1,512,2048]{2,1,0:T(8,128)(2,1)}, u32[]{:S(2)}) copy-start(bf16[1,512,2048]{2,1,0:T(8,128)(2,1)} %param.27) | copy-start | bytes 6291460
  0.0 68.0 %collective-permute-start.1 = (bf16[512,2048]{1,0:T(8,128)(2,1)}, bf16[512,2048]{1,0:T(8,128)(2,1)}, u32[]{:S(2)}, u32[]{:S(2)}) collective-permute-start(bf16[512,2048]{1,0:T(8,128)(2,1)} %own_weight.1), channel_id=1, source_target_pairs={{0,1},{1,0},{2,3},{3,2},{4,5},{5,4},{6,7},{7,6},{8,9},{9,8},{10,11... | collective-permute-start | bytes 6291464 | tf_op jit(solution)/shard_map/ppermute | solution.py:451
  14.3 23.7 %all-to-all-start = ((bf16[8,192,128]{2,1,0:T(8,128)(2,1)}), bf16[8,192,128]{2,1,0:T(8,128)(2,1)S(1)}, u32[]{:S(2)}, u32[]{:S(2)}) async-start(bf16[8,192,128]{2,1,0:T(8,128)(2,1)} %get-tuple-element.23), calls=%async_computation | async-start | bytes 786432 | tf_op jit(solution)/shard_map/all_to_all | solution.py:464
  31.0 31.2 %copy-start.10 = (f32[128]{0:T(128)S(1)}, f32[128]{0:T(128)}, u32[]{:S(2)}) copy-start(f32[128]{0:T(128)} %param.21) | copy-start | bytes 1540
  31.6 0.9 copy-start.4
  39.0 0.7 copy-start.3
  39.7 9.7 %all-to-all-start.1 = ((bf16[4,192,128]{2,1,0:T(8,128)(2,1)}), bf16[4,192,128]{2,1,0:T(8,128)(2,1)S(1)}, u32[]{:S(2)}, u32[]{:S(2)}) async-start(bf16[4,192,128]{2,1,0:T(8,128)(2,1)} %copy-done.3), calls=%async_computation.1 | async-start | bytes 393216 | tf_op jit(solution)/shard_map/all_to_all | solution.py:472
  49.4 18.6 %copy-start.1 = (bf16[512,2048]{1,0:T(8,128)(2,1)S(1)}, bf16[512,2048]{1,0:T(8,128)(2,1)}, u32[]{:S(2)}) copy-start(bf16[512,2048]{1,0:T(8,128)(2,1)} %own_weight.1) | copy-start | bytes 6291460
  62.1 1.2 copy-start.2
  63.4 1.0 copy-start.6
  64.4 1.0 copy-start.7
  66.4 1.6 collective-permute-start
  68.0 23.5 %copy-start.8 = (bf16[64,2048]{1,0:T(8,128)(2,1)S(1)}, bf16[64,2048]{1,0:T(8,128)(2,1)}, u32[]{:S(2)}) copy-start(bf16[64,2048]{1,0:T(8,128)(2,1)} %hidden_ref.1) | copy-start | bytes 786436
  68.0 23.5 %copy-start.9 = (f32[2048]{0:T(1024)S(1)}, f32[2048]{0:T(1024)}, u32[]{:S(2)}) copy-start(f32[2048]{0:T(1024)} %param.23) | copy-start | bytes 24580
  71.7 39.4 %copy-start.5 = (bf16[768,512]{1,0:T(8,128)(2,1)S(1)}, bf16[768,512]{1,0:T(8,128)(2,1)}, u32[]{:S(2)}) copy-start(bf16[768,512]{1,0:T(8,128)(2,1)} %copy-done.4) | copy-start | bytes 2359300
  108.5 2.7 collective-permute-start.2
  113.8 76.1 %copy-start.11 = (bf16[1,2048,1024]{2,1,0:T(8,128)(2,1)S(1)}, bf16[1,2048,1024]{2,1,0:T(8,128)(2,1)}, u32[]{:S(2)}) copy-start(bf16[1,2048,1024]{2,1,0:T(8,128)(2,1)} %param.26) | copy-start | bytes 12582916
  275.4 2.7 collective-permute-start.3

commit v3 on v2

--- a/solution.py
+++ b/solution.py
@@ -94,34 +94,39 @@
             [jnp.broadcast_to(cum[BLOCK - 1 : BLOCK, h : h + 1], (BLOCK, 1)) for h in range(HEADS)]
         )
         strict = jnp.logical_and(same, row > col)
-        spread = jnp.where(strict, cum_col - as_row(cum_col, row, col), 0.0)
-        power = jnp.where(
-            strict,
-            -(jnp.exp(spread) * mm_t(keys, keys)) * ((rate_col * scale) * as_row(scale, row, col)),
-            0.0,
-        )
+        past = jnp.exp(cum_col) * scale
+        onward = as_row(jnp.exp(-cum_col) * scale, row, col)
+        power = jnp.where(strict, mm_t(keys, keys) * ((-rate_col * past) * onward), 0.0)
         raw = value_ref[rows, :]
         wide = keys.astype(f32)
         answer = jnp.concatenate(
             [
                 rate_col * stack_rows([raw[:, h * DV : (h + 1) * DV] for h in range(HEADS)]).astype(f32),
-                (rate_col * jnp.exp(cum_col) * scale) * wide,
+                (rate_col * past) * wide,
             ],
             axis=1,
         )
-        reach = 1
-        while reach < BLOCK:
-            answer = answer + mm(power, answer)
-            reach *= 2
-            if reach < BLOCK:
-                power = mm(power, power)
+        return rows, power, answer, (jnp.exp(last_col - cum_col) * scale) * wide
+
+    def finish(b, answer, tail):
         values_s[b] = answer[:, :DV]
         values_ref[b] = answer[:, :DV].astype(bf16)
         inner_ref[b] = answer[:, DV:].astype(bf16)
-        tail_s[b] = ((jnp.exp(last_col - cum_col) * scale) * wide).astype(bf16)
-
-    for b in range(blocks):
-        one_block(b)
+        tail_s[b] = tail.astype(bf16)
+
+    for first in range(0, blocks, 4):
+        group = range(first, first + 4)
+        made = [one_block(b) for b in group]
+        powers = [m[1] for m in made]
+        answers = [m[2] for m in made]
+        reach = 1
+        while reach < BLOCK:
+            answers = [a + mm(p, a) for p, a in zip(powers, answers)]
+            reach *= 2
+            if reach < BLOCK:
+                powers = [mm(p, p) for p in powers]
+        for b, a, m in zip(group, answers, made):
+            finish(b, a, m[3])
 
     place = lax.broadcasted_iota(jnp.int32, (DK, DV + DK), 0)
     lane_place = lax.broadcasted_iota(jnp.int32, (DK, DV + DK), 1)
@@ -130,14 +135,18 @@
 
     def advance(b, carry):
         last = cum_ref[pl.ds(b * BLOCK + BLOCK - 1, 1), :]
+        parts = [slice(h * BLOCK, (h + 1) * BLOCK) for h in range(HEADS)]
+        states = [state_s[h] for h in range(HEADS)]
+        rounded = [state.astype(bf16) for state in states]
+        changes = [mm(inner_ref[b, part, :], now) for part, now in zip(parts, rounded)]
+        given = [
+            jnp.concatenate([values_s[b, part, :] - change[:, :DV], -change[:, DV:]], axis=1)
+            for part, change in zip(parts, changes)
+        ]
+        added = [t_mm(tail_s[b, part, :], rows) for part, rows in zip(parts, given)]
         for h in range(HEADS):
-            part = slice(h * BLOCK, (h + 1) * BLOCK)
-            state = state_s[h]
-            rounded = state.astype(bf16)
-            starts_ref[b, h] = rounded
-            change = mm(inner_ref[b, part, :], rounded)
-            given = jnp.concatenate([values_s[b, part, :] - change[:, :DV], -change[:, DV:]], axis=1)
-            state_s[h] = jnp.exp(last[:, h : h + 1]) * state + t_mm(tail_s[b, part, :], given)
+            starts_ref[b, h] = rounded[h]
+            state_s[h] = jnp.exp(last[:, h : h + 1]) * states[h] + added[h]
         return carry
 
     lax.fori_loop(0, blocks, advance, 0, unroll=True)
@@ -185,14 +194,11 @@
         query_scale = query_scale * DK ** (-0.5)
         cum_col = head_column(cum_ref[rows, :])
         inclusive = jnp.logical_and(same, row >= col)
-        spread = jnp.where(inclusive, cum_col - as_row(cum_col, row, col), 0.0)
-        attention = jnp.where(
-            inclusive,
-            jnp.exp(spread) * mm_t(queries, keys) * (query_scale * as_row(scale, row, col)),
-            0.0,
-        )
+        past = jnp.exp(cum_col) * query_scale
+        onward = as_row(jnp.exp(-cum_col) * scale, row, col)
+        attention = jnp.where(inclusive, mm_t(queries, keys) * (past * onward), 0.0)
         both = mm(attention, jnp.concatenate([values_ref[b], inner_ref[b]], axis=1))
-        emitter = ((jnp.exp(cum_col) * query_scale) * queries.astype(f32) - both[:, DV:]).astype(bf16)
+        emitter = (past * queries.astype(f32) - both[:, DV:]).astype(bf16)
         for h in range(HEADS):
             part = slice(h * BLOCK, (h + 1) * BLOCK)
             read = mm(emitter[part, :], starts_ref[b, h])
@@ -268,21 +274,22 @@
     )(row, totals, maps)
 
 
-def gated_kernel(core_side, core_ref, reach_ref, start_ref, gate_ref, gain_ref, own_ref, other_ref):
-    tokens = core_ref.shape[0]
-    share = tokens // LOCAL
+def gated_kernel(
+    core_side, core_ref, reach_ref, start_ref, gate_ref, gain_ref, own_ref, other_ref, gated_s
+):
+    share = core_ref.shape[0] // LOCAL
+    lanes = [slice(h * DV, (h + 1) * DV) for h in range(HEADS)]
+    reads = [mm_t(reach_ref[:, lane], start_ref[lane, :]) for lane in lanes]
+    for lane, read in zip(lanes, reads):
+        core = core_ref[:, lane] + read
+        core = core * lax.rsqrt(jnp.mean(core * core, axis=-1, keepdims=True) + 1e-06)
+        gate = gate_ref[:, lane].astype(f32)
+        gated_s[:, lane] = (core * gain_ref[...] * (gate / (1.0 + jnp.exp(-gate)))).astype(bf16)
     side = core_side[0]
     for chip in range(LOCAL // 2):
         for ref, parity in ((own_ref, side), (other_ref, 1 - side)):
-            rows = pl.ds((2 * chip + parity) * share, share)
-            for h in range(HEADS):
-                lanes = slice(h * DV, (h + 1) * DV)
-                core = core_ref[rows, lanes] + mm_t(reach_ref[rows, lanes], start_ref[lanes, :])
-                core = core * lax.rsqrt(jnp.mean(core * core, axis=-1, keepdims=True) + 1e-06)
-                gate = gate_ref[rows, lanes].astype(f32)
-                ref[chip * share : (chip + 1) * share, lanes] = (
-                    core * gain_ref[...] * (gate / (1.0 + jnp.exp(-gate)))
-                ).astype(bf16)
+            first = pl.multiple_of((2 * chip + parity) * share, share)
+            ref[chip * share : (chip + 1) * share, :] = gated_s[pl.ds(first, share), :]
 
 
 def gated_halves(side, core, reach, starts, gate, gain):
@@ -294,7 +301,8 @@
         out_shape=(half, half),
         in_specs=[pl.BlockSpec(memory_space=pltpu.SMEM)] + [vmem] * 5,
         out_specs=(vmem, vmem),
-        compiler_params=pltpu.CompilerParams(vmem_limit_bytes=32 * 2**20),
+        scratch_shapes=[pltpu.VMEM((tokens, HEADS * DV), bf16)],
+        compiler_params=pltpu.CompilerParams(vmem_limit_bytes=60 * 2**20),
         name="gated_halves",
     )(side, core, reach, starts, gate, gain)
 
@@ -306,7 +314,7 @@
 def project(own, other, own_weight, other_weight):
     rows, depth = own.shape
     width = own_weight.shape[1]
-    tile = 512
+    tile = width // 2
     rows_spec = pl.BlockSpec((rows, depth), lambda i: (0, 0))
     weight_spec = pl.BlockSpec((depth, tile), lambda i: (0, i))
     return pl.pallas_call(
@@ -315,7 +323,7 @@
         grid=(width // tile,),
         in_specs=[rows_spec, rows_spec, weight_spec, weight_spec],
         out_specs=pl.BlockSpec((rows, tile), lambda i: (0, i)),
-        compiler_params=pltpu.CompilerParams(vmem_limit_bytes=32 * 2**20),
+        compiler_params=pltpu.CompilerParams(vmem_limit_bytes=60 * 2**20),
         name="project",
     )(own, other, own_weight, other_weight)
 
@@ -406,7 +414,7 @@
 def pick_rows(pick, own, other):
     slots, tokens = pick.shape
     half, width = own.shape
-    tile = 512
+    tile = 1024
     half_spec = pl.BlockSpec((half, tile), lambda i: (0, i))
     return pl.pallas_call(
         pick_kernel,
@@ -423,28 +431,24 @@
     out_ref[...] = mm(merge_ref[...], rows_ref[...]).astype(bf16)
 
 
-def merge_add_kernel(merge_ref, rows_ref, add_ref, out_ref):
-    out_ref[...] = (mm(merge_ref[...], rows_ref[...]) + add_ref[...].astype(f32)).astype(bf16)
-
-
-def merge_rows(merge, half, rows, *add):
+def merge_rows(merge, half, rows):
     tokens, slots = merge.shape
     width = rows.shape[1]
-    tile = 512
-    out_spec = pl.BlockSpec((tokens // 2, tile), lambda i: (0, i))
-    return pl.pallas_call(
-        merge_add_kernel if add else merge_kernel,
+    return pl.pallas_call(
+        merge_kernel,
         out_shape=jax.ShapeDtypeStruct((tokens // 2, width), bf16),
-        grid=(width // tile,),
+        grid=(1,),
         in_specs=[
             pl.BlockSpec((tokens // 2, slots), lambda i: (half, 0)),
-            pl.BlockSpec((slots, tile), lambda i: (0, i)),
-        ]
-        + [out_spec] * len(add),
-        out_specs=out_spec,
+            pl.BlockSpec((slots, width), lambda i: (0, 0)),
+        ],
+        out_specs=pl.BlockSpec((tokens // 2, width), lambda i: (0, 0)),
         compiler_params=pltpu.CompilerParams(vmem_limit_bytes=32 * 2**20),
+        cost_estimate=pl.CostEstimate(
+            flops=tokens * slots * width, bytes_accessed=5 * 10**6, transcendentals=0
+        ),
         name="merge_rows",
-    )(merge, rows, *add)
+    )(merge, rows)
 
 
 def swap_cores(array):
@@ -528,7 +532,8 @@
         node_count * capacity, width
     )
     given = swap_cores(merge_rows(merge, 1, returned))
-    summed = merge_rows(merge, 0, returned, given)
+    kept = merge_rows(merge, 0, returned)
+    summed = (kept.astype(f32) + given.astype(f32)).astype(bf16)
     arrived = across_chips(summed.reshape(chips, share, width))
     return (hidden_state + jnp.sum(arrived.astype(f32), axis=0)).astype(bf16)
 

time: 302 us -> 296 us (0.980)
  Pallas kernels: 34.7 us -> 30.9 us
    pallas_call x1, Pallas kernels: 14.3 us -> 10.2 us  [shard_maps(): pl.pallas_call(maps_kernel, out_shape=(jax.ShapeDtypeStruct((HEADS * SPLI...]
where the time goes in v3:
time: 296 us; the launch traced here: 293 us
  blocking collectives  221 us (75%)
  Pallas kernels  30.9 us (10%)
  waiting for transfers between devices  16.5 us (6%)
  starting transfers between devices  13.4 us (5%)
  matrix products  5.24 us (2%)
  local copies, waits for them, and re-layouts  4.15 us (1%)
    all_to_all x2, blocking collectives, across_nodes(): lax.all_to_all(array, 'node', split_axis=0, concat_axis=0, tiled=True)  154 us
    all_to_all x3, blocking collectives, across_chips(): lax.all_to_all(array, 'local', split_axis=0, concat_axis=0, tiled=True, a...  54.8 us
    all_to_all x1, blocking collectives, along_row(): lax.all_to_all(array, 'node', split_axis=0, concat_axis=0, tiled=True, ax...  12.1 us
    pallas_call x1, Pallas kernels, shard_maps(): pl.pallas_call(maps_kernel, out_shape=(jax.ShapeDtypeStruct((HEADS * SPLI...  10.2 us
    all_to_all x1, starting transfers between devices, along_row(): lax.all_to_all(array, 'node', split_axis=0, concat_axis=0, tiled=True, ax...  8.48 us
    pallas_call x1, Pallas kernels, block_reads(): pl.pallas_call(reads_kernel, out_shape=(jax.ShapeDtypeStruct((tokens, HEA...  6.16 us
    ppermute x4, waiting for transfers between devices, swap_cores(): return lax.ppermute(array, 'local', [(i, i ^ 1) for i in range(LOCAL)])  6.06 us
  transfers between devices with their start and end apart: 6, of which 5 were waited for; matrix products, arithmetic and copies ran while one was open for 1% of the time, Pallas kernels for 8%

profile of v3, /device:TPU:2, one launch (start us, length us, event | category | flops | bytes accessed | tf_op | source)
XLA Modules:
  0.0 293.0 jit_solution(12784626876951455016)
XLA Ops:
  0.0 10.2 %shard_maps.1 = (bf16[8,192,128]{2,1,0:T(8,128)(2,1)}, f32[512,4]{1,0:T(8,128)}, bf16[8,256,128]{2,1,0:T(8,128)(2,1)}, bf16[8,256,128]{2,1,0:T(8,128)(2,1)}, bf16[8,4,128,256]{3,2,1,0:T(8,128)(2,1)}) custom-call(bf16[512,256]{1,0:T(8,128)(2,1)} %key_ref.3, bf16[512,512]{1,0:T(8,128)(2,1)} %value_ref.1, f32[4,512]{1,0:T(4,128)} %bitcast.41, f32[4,512]{1,0:T(4,128)} %bitcast.42), custom_call_target="tpu_custom_call" | custom-call | tf_op jit(solution)/shard_map/shard_maps/pallas_call | solution.py:166
  10.2 8.5 %all-to-all-start = ((bf16[8,192,128]{2,1,0:T(8,128)(2,1)}), bf16[8,192,128]{2,1,0:T(8,128)(2,1)S(1)}, u32[]{:S(2)}, u32[]{:S(2)}) async-start(bf16[8,192,128]{2,1,0:T(8,128)(2,1)} %get-tuple-element.23), calls=%async_computation | async-start | bytes 786432 | tf_op jit(solution)/shard_map/all_to_all | solution.py:468
  20.6 6.2 %block_reads.1 = (f32[512,512]{1,0:T(8,128)}, bf16[512,512]{1,0:T(8,128)(2,1)}) custom-call(bf16[512,256]{1,0:T(8,128)(2,1)} %query_ref.1, bf16[512,256]{1,0:T(8,128)(2,1)} %key_ref.3, f32[512,4]{1,0:T(8,128)} %get-tuple-element.24.cum_ref, bf16[8,256,128]{2,1,0:T(8,128)(2,1)} %get-tuple-element.25.inner_ref, ...), custom_call_target="tpu_custom_call" | custom-call | flops 2000000000 | bytes 8000000 | tf_op jit(solution)/shard_map/block_reads/pallas_call | solution.py:214
  28.3 5.6 %all-to-all-done.maps_ref = bf16[8,192,128]{2,1,0:T(8,128)(2,1)S(1)} async-done(((bf16[8,192,128]{2,1,0:T(8,128)(2,1)}), bf16[8,192,128]{2,1,0:T(8,128)(2,1)S(1)}, u32[]{:S(2)}, u32[]{:S(2)}) %all-to-all-start) | async-done | bytes 393248 | tf_op jit(solution)/shard_map/all_to_all | solution.py:468
  33.8 1.0 row_total.1
  35.6 4.8 %all-to-all-start.1 = ((bf16[4,192,128]{2,1,0:T(8,128)(2,1)}), bf16[4,192,128]{2,1,0:T(8,128)(2,1)S(1)}, u32[]{:S(2)}, u32[]{:S(2)}) async-start(bf16[4,192,128]{2,1,0:T(8,128)(2,1)} %copy-done.1), calls=%async_computation.1 | async-start | bytes 393216 | tf_op jit(solution)/shard_map/all_to_all | solution.py:476
  40.4 4.9 %all-to-all-done.1.totals_ref = bf16[4,192,128]{2,1,0:T(8,128)(2,1)S(1)} async-done(((bf16[4,192,128]{2,1,0:T(8,128)(2,1)}), bf16[4,192,128]{2,1,0:T(8,128)(2,1)S(1)}, u32[]{:S(2)}, u32[]{:S(2)}) %all-to-all-start.1) | async-done | bytes 196640 | tf_op jit(solution)/shard_map/all_to_all | solution.py:476
  45.3 1.3 shard_starts.1
  46.5 12.1 %all_to_all.40 = bf16[8,64,128]{2,1,0:T(8,128)(2,1)} all-to-all(bf16[8,64,128]{2,1,0:T(8,128)(2,1)S(1)} %shard_starts.1), channel_id=1, replica_groups={{0,8,16,24,32,40,48,56},{64,72,80,88,96,104,112,120},{128,136,144,152,1..., dimensions={0} | all-to-all | bytes 262144 | tf_op jit(solution)/shard_map/all_to_all | solution.py:468
  58.7 3.1 %gated_halves.1 = (bf16[256,512]{1,0:T(8,128)(2,1)}, bf16[256,512]{1,0:T(8,128)(2,1)}) custom-call(s32[1]{0:T(128)} %bitcast.core_side, f32[512,512]{1,0:T(8,128)} %get-tuple-element.32.core_ref, bf16[512,512]{1,0:T(8,128)(2,1)} %get-tuple-element.33.reach_ref, bf16[512,128]{1,0:T(8,128)(2,1)} %bitcast.38, bf16[512,512]{1,0:T(8,128)(2,1)} %gate_ref.1, ...), custom_call_target="tpu_custom_call" | custom-call | tf_op jit(solution)/shard_map/gated_halves/pallas_call | solution.py:299
  61.8 1.7 collective-permute-done.other_ref
  64.2 3.9 %project.1 = bf16[256,2048]{1,0:T(8,128)(2,1)} custom-call(bf16[256,512]{1,0:T(8,128)(2,1)} %get-tuple-element.35.own_ref, bf16[256,512]{1,0:T(8,128)(2,1)} %copy-done.6, bf16[512,2048]{1,0:T(8,128)(2,1)} %own_weight.1, bf16[512,2048]{1,0:T(8,128)(2,1)} %collective-permute-done.1.other_weight), custom_call_target="tpu_custom_call" | custom-call | tf_op jit(solution)/shard_map/project/pallas_call | solution.py:320
  68.1 20.0 %all_to_all.41.parts_ref = bf16[4,64,2048]{2,1,0:T(8,128)(2,1)S(1)} all-to-all(bf16[4,64,2048]{2,1,0:T(8,128)(2,1)} %bitcast.35), channel_id=1, replica_groups={{0,2,4,6},{1,3,5,7},{8,10,12,14},{9,11,13,15},{16,18,20,22},{17,19,21,2..., dimensions={0} | all-to-all | bytes 2097152 | tf_op jit(solution)/shard_map/all_to_all | solution.py:460
  88.5 16.7 %all_to_all.42 = bf16[4,64,2048]{2,1,0:T(8,128)(2,1)S(1)} all-to-all(bf16[4,64,2048]{2,1,0:T(8,128)(2,1)S(1)} %get-tuple-element.40), channel_id=1, replica_groups={{0,2,4,6},{1,3,5,7},{8,10,12,14},{9,11,13,15},{16,18,20,22},{17,19,21,2..., dimensions={0} | all-to-all | bytes 2097152 | tf_op jit(solution)/shard_map/all_to_all | solution.py:460
  105.1 2.7 collective-permute-done.2.other_ref
  107.8 2.3 pick_rows.1
  110.1 76.0 %all_to_all.43 = bf16[32,24,2048]{2,1,0:T(8,128)(2,1)S(1)} all-to-all(bf16[32,24,2048]{2,1,0:T(8,128)(2,1)S(1)} %bitcast.30), channel_id=1, replica_groups=mesh['node'=32,'local'=8] {'node'}, dimensions={0} | all-to-all | bytes 6291456 | tf_op jit(solution)/shard_map/all_to_all | solution.py:482
  186.2 3.4 %fusion = f32[768,1024]{1,0:T(8,128)S(1)} fusion(bf16[768,2048]{1,0:T(8,128)(2,1)S(1)} %bitcast.36, bf16[1,2048,1024]{2,1,0:T(8,128)(2,1)S(1)} %copy-done.7), kind=kOutput, calls=%fused_computation | convolution fusion | flops 3221225472 | bytes 10485760 | tf_op jit(solution)/shard_map/dot_general | solution.py:527
  189.6 1.8 convolution_convert_fusion
  191.4 78.4 %all_to_all.44 = bf16[32,24,2048]{2,1,0:T(8,128)(2,1)S(1)} all-to-all(bf16[32,24,2048]{2,1,0:T(8,128)(2,1)S(1)} %bitcast.37), channel_id=1, replica_groups=mesh['node'=32,'local'=8] {'node'}, dimensions={0} | all-to-all | bytes 6291456 | tf_op jit(solution)/shard_map/all_to_all | solution.py:482
  269.9 1.0 merge_rows.3
  271.0 1.0 merge_rows.2
  272.0 1.7 collective-permute-done.3
  274.0 18.1 %all_to_all.45 = bf16[4,64,2048]{2,1,0:T(8,128)(2,1)S(1)} all-to-all(bf16[4,64,2048]{2,1,0:T(8,128)(2,1)S(1)} %bitcast.34), channel_id=1, replica_groups={{0,2,4,6},{1,3,5,7},{8,10,12,14},{9,11,13,15},{16,18,20,22},{17,19,21,2..., dimensions={0} | all-to-all | bytes 2097152 | tf_op jit(solution)/shard_map/all_to_all | solution.py:460
  (34 shorter events, 6.5 us)
Async XLA Ops:
  0.0 189.6 %copy-start = (bf16[1,512,2048]{2,1,0:T(8,128)(2,1)S(1)}, bf16[1,512,2048]{2,1,0:T(8,128)(2,1)}, u32[]{:S(2)}) copy-start(bf16[1,512,2048]{2,1,0:T(8,128)(2,1)} %param.27) | copy-start | bytes 6291460
  0.0 63.5 %collective-permute-start.1 = (bf16[512,2048]{1,0:T(8,128)(2,1)}, bf16[512,2048]{1,0:T(8,128)(2,1)}, u32[]{:S(2)}, u32[]{:S(2)}) collective-permute-start(bf16[512,2048]{1,0:T(8,128)(2,1)} %own_weight.1), channel_id=1, source_target_pairs={{0,1},{1,0},{2,3},{3,2},{4,5},{5,4},{6,7},{7,6},{8,9},{9,8},{10,11... | collective-permute-start | bytes 6291464 | tf_op jit(solution)/shard_map/ppermute | solution.py:455
  10.2 23.7 %all-to-all-start = ((bf16[8,192,128]{2,1,0:T(8,128)(2,1)}), bf16[8,192,128]{2,1,0:T(8,128)(2,1)S(1)}, u32[]{:S(2)}, u32[]{:S(2)}) async-start(bf16[8,192,128]{2,1,0:T(8,128)(2,1)} %get-tuple-element.23), calls=%async_computation | async-start | bytes 786432 | tf_op jit(solution)/shard_map/all_to_all | solution.py:468
  27.4 0.9 copy-start.2
  34.9 0.7 copy-start.1
  35.6 9.7 %all-to-all-start.1 = ((bf16[4,192,128]{2,1,0:T(8,128)(2,1)}), bf16[4,192,128]{2,1,0:T(8,128)(2,1)S(1)}, u32[]{:S(2)}, u32[]{:S(2)}) async-start(bf16[4,192,128]{2,1,0:T(8,128)(2,1)} %copy-done.1), calls=%async_computation.1 | async-start | bytes 393216 | tf_op jit(solution)/shard_map/all_to_all | solution.py:476
  61.8 1.7 collective-permute-start
  63.5 0.7 copy-start.6
  68.1 20.0 %copy-start.4 = (bf16[64,2048]{1,0:T(8,128)(2,1)S(1)}, bf16[64,2048]{1,0:T(8,128)(2,1)}, u32[]{:S(2)}) copy-start(bf16[64,2048]{1,0:T(8,128)(2,1)} %hidden_ref.1) | copy-start | bytes 786436
  68.1 20.0 %copy-start.5 = (f32[2048]{0:T(1024)S(1)}, f32[2048]{0:T(1024)}, u32[]{:S(2)}) copy-start(f32[2048]{0:T(1024)} %param.23) | copy-start | bytes 24580
  88.2 19.6 %copy-start.3 = (bf16[768,512]{1,0:T(8,128)(2,1)S(1)}, bf16[768,512]{1,0:T(8,128)(2,1)}, u32[]{:S(2)}) copy-start(bf16[768,512]{1,0:T(8,128)(2,1)} %copy-done.2) | copy-start | bytes 2359300
  105.1 2.7 collective-permute-start.2
  110.1 76.1 %copy-start.7 = (bf16[1,2048,1024]{2,1,0:T(8,128)(2,1)S(1)}, bf16[1,2048,1024]{2,1,0:T(8,128)(2,1)}, u32[]{:S(2)}) copy-start(bf16[1,2048,1024]{2,1,0:T(8,128)(2,1)} %param.26) | copy-start | bytes 12582916
  270.9 2.7 collective-permute-start.3

commit v4 on v3

--- a/solution.py
+++ b/solution.py
@@ -275,8 +275,11 @@
 
 
 def gated_kernel(
-    core_side, core_ref, reach_ref, start_ref, gate_ref, gain_ref, own_ref, other_ref, gated_s
+    core_side, core_ref, reach_ref, start_ref, gate_ref, gain_ref, weight_hbm,
+    own_ref, part_ref, gated_s, other_s, weight_s, arrival,
 ):
+    fetch = pltpu.make_async_copy(weight_hbm, weight_s, arrival)
+    fetch.start()
     share = core_ref.shape[0] // LOCAL
     lanes = [slice(h * DV, (h + 1) * DV) for h in range(HEADS)]
     reads = [mm_t(reach_ref[:, lane], start_ref[lane, :]) for lane in lanes]
@@ -287,45 +290,52 @@
         gated_s[:, lane] = (core * gain_ref[...] * (gate / (1.0 + jnp.exp(-gate)))).astype(bf16)
     side = core_side[0]
     for chip in range(LOCAL // 2):
-        for ref, parity in ((own_ref, side), (other_ref, 1 - side)):
+        for ref, parity in ((own_ref, side), (other_s, 1 - side)):
             first = pl.multiple_of((2 * chip + parity) * share, share)
             ref[chip * share : (chip + 1) * share, :] = gated_s[pl.ds(first, share), :]
-
-
-def gated_halves(side, core, reach, starts, gate, gain):
-    tokens = core.shape[0]
+    fetch.wait()
+    part_ref[...] = mm(other_s[...], weight_s[...]).astype(bf16)
+
+
+def gated_part(side, core, reach, starts, gate, gain, weight):
+    tokens, depth = core.shape
+    half = tokens // 2
     vmem = pl.BlockSpec(memory_space=pltpu.VMEM)
-    half = jax.ShapeDtypeStruct((tokens // 2, HEADS * DV), bf16)
     return pl.pallas_call(
         gated_kernel,
-        out_shape=(half, half),
-        in_specs=[pl.BlockSpec(memory_space=pltpu.SMEM)] + [vmem] * 5,
+        out_shape=(
+            jax.ShapeDtypeStruct((half, depth), bf16),
+            jax.ShapeDtypeStruct((half, weight.shape[1]), bf16),
+        ),
+        in_specs=[pl.BlockSpec(memory_space=pltpu.SMEM)]
+        + [vmem] * 5
+        + [pl.BlockSpec(memory_space=pl.ANY)],
         out_specs=(vmem, vmem),
-        scratch_shapes=[pltpu.VMEM((tokens, HEADS * DV), bf16)],
+        scratch_shapes=[
+            pltpu.VMEM((tokens, depth), bf16),
+            pltpu.VMEM((half, depth), bf16),
+            pltpu.VMEM(weight.shape, bf16),
+            pltpu.SemaphoreType.DMA,
+        ],
         compiler_params=pltpu.CompilerParams(vmem_limit_bytes=60 * 2**20),
-        name="gated_halves",
-    )(side, core, reach, starts, gate, gain)
-
-
-def project_kernel(own_ref, other_ref, own_weight, other_weight, out_ref):
-    out_ref[...] = (mm(own_ref[...], own_weight[...]) + mm(other_ref[...], other_weight[...])).astype(bf16)
-
-
-def project(own, other, own_weight, other_weight):
-    rows, depth = own.shape
-    width = own_weight.shape[1]
-    tile = width // 2
-    rows_spec = pl.BlockSpec((rows, depth), lambda i: (0, 0))
-    weight_spec = pl.BlockSpec((depth, tile), lambda i: (0, i))
+        name="gated_part",
+    )(side, core, reach, starts, gate, gain, weight)
+
+
+def project_kernel(rows_ref, weight_ref, out_ref):
+    out_ref[...] = mm(rows_ref[...], weight_ref[...]).astype(bf16)
+
+
+def project(rows, weight):
     return pl.pallas_call(
         project_kernel,
-        out_shape=jax.ShapeDtypeStruct((rows, width), bf16),
-        grid=(width // tile,),
-        in_specs=[rows_spec, rows_spec, weight_spec, weight_spec],
-        out_specs=pl.BlockSpec((rows, tile), lambda i: (0, i)),
-        compiler_params=pltpu.CompilerParams(vmem_limit_bytes=60 * 2**20),
+        out_shape=jax.ShapeDtypeStruct((rows.shape[0], weight.shape[1]), bf16),
+        compiler_params=pltpu.CompilerParams(vmem_limit_bytes=32 * 2**20),
+        cost_estimate=pl.CostEstimate(
+            flops=2 * rows.size * weight.shape[1], bytes_accessed=4 * 10**6, transcendentals=0
+        ),
         name="project",
-    )(own, other, own_weight, other_weight)
+    )(rows, weight)
 
 
 def residual_kernel(parts_ref, hidden_ref, gain_ref, state_ref, normed_ref):
@@ -496,8 +506,6 @@
     capacity = 6 * tokens * top // (5 * node_count * LOCAL)
     side_array = side.astype(jnp.int32).reshape(1)
 
-    other_weight = swap_cores(out_weight)
-
     def by_side(array):
         split = array.T.reshape(top, chips, 2, share)
         split = jnp.where(side == 0, split, split[:, :, ::-1])
@@ -515,10 +523,12 @@
     totals = across_rows(row_total(maps, node_count // NODE_ROW))
     row = (lax.axis_index("node") // NODE_ROW).astype(jnp.int32).reshape(1)
     carried = along_row(shard_starts(row, totals, maps)).reshape(HEADS * DV, DK)
-    own_half, other_half = gated_halves(
-        side_array, core, reach, carried, out_gate, norm_gain.reshape(1, DV)
-    )
-    partial = project(own_half, swap_cores(other_half), out_weight, other_weight)
+    own_half, other_part = gated_part(
+        side_array, core, reach, carried, out_gate, norm_gain.reshape(1, DV), out_weight
+    )
+    given_part = swap_cores(other_part)
+    kept_part = project(own_half, out_weight)
+    partial = (kept_part.astype(f32) + given_part.astype(f32)).astype(bf16)
     parts = across_chips(partial.reshape(chips, share, width))
     hidden_state, normed = residual(parts, hidden_in, post_gain.reshape(1, width))
     own_rows = across_chips(normed).reshape(chips * share, width)

time: 296 us -> 296 us (level)
    ppermute x4 -> x3, waiting for transfers between devices: 6.06 us -> 4.32 us  [swap_cores(): return lax.ppermute(array, 'local', [(i, i ^ 1) for i in range(LOCAL)])]
  transfers between devices with their start and end apart: 6 -> 5, of which waited for: 5 -> 4; matrix products, arithmetic and copies ran while one was open for 1% -> 1% of each run, Pallas kernels for 8% -> 3%
where the time goes in v4:
time: 296 us; the launch traced here: 293 us
  blocking collectives  222 us (75%)
  Pallas kernels  29.3 us (10%)
  waiting for transfers between devices  14.3 us (5%)
  starting transfers between devices  13.7 us (5%)
  local copies, waits for them, and re-layouts  6.04 us (2%)
  matrix products  5.24 us (2%)
    all_to_all x2, blocking collectives, across_nodes(): lax.all_to_all(array, 'node', split_axis=0, concat_axis=0, tiled=True)  154 us
    all_to_all x3, blocking collectives, across_chips(): lax.all_to_all(array, 'local', split_axis=0, concat_axis=0, tiled=True, a...  55.5 us
    all_to_all x1, blocking collectives, along_row(): lax.all_to_all(array, 'node', split_axis=0, concat_axis=0, tiled=True, ax...  12.1 us
    pallas_call x1, Pallas kernels, shard_maps(): pl.pallas_call(maps_kernel, out_shape=(jax.ShapeDtypeStruct((HEADS * SPLI...  10.1 us
    all_to_all x1, starting transfers between devices, along_row(): lax.all_to_all(array, 'node', split_axis=0, concat_axis=0, tiled=True, ax...  8.47 us
    pallas_call x1, Pallas kernels, block_reads(): pl.pallas_call(reads_kernel, out_shape=(jax.ShapeDtypeStruct((tokens, HEA...  6.12 us
  transfers between devices with their start and end apart: 5, of which 4 were waited for; matrix products, arithmetic and copies ran while one was open for 1% of the time, Pallas kernels for 3%

profile of v4, /device:TPU:2, one launch (start us, length us, event | category | flops | bytes accessed | tf_op | source)
XLA Modules:
  0.0 292.6 jit_solution(12446347138576118637)
XLA Ops:
  0.0 10.1 %shard_maps.1 = (bf16[8,192,128]{2,1,0:T(8,128)(2,1)}, f32[512,4]{1,0:T(8,128)}, bf16[8,256,128]{2,1,0:T(8,128)(2,1)}, bf16[8,256,128]{2,1,0:T(8,128)(2,1)}, bf16[8,4,128,256]{3,2,1,0:T(8,128)(2,1)}) custom-call(bf16[512,256]{1,0:T(8,128)(2,1)} %key_ref.3, bf16[512,512]{1,0:T(8,128)(2,1)} %value_ref.1, f32[4,512]{1,0:T(4,128)} %bitcast.41, f32[4,512]{1,0:T(4,128)} %bitcast.42), custom_call_target="tpu_custom_call" | custom-call | tf_op jit(solution)/shard_map/shard_maps/pallas_call | solution.py:166
  10.1 8.5 %all-to-all-start = ((bf16[8,192,128]{2,1,0:T(8,128)(2,1)}), bf16[8,192,128]{2,1,0:T(8,128)(2,1)S(1)}, u32[]{:S(2)}, u32[]{:S(2)}) async-start(bf16[8,192,128]{2,1,0:T(8,128)(2,1)} %get-tuple-element.23), calls=%async_computation | async-start | bytes 786432 | tf_op jit(solution)/shard_map/all_to_all | solution.py:478
  20.6 6.1 %block_reads.1 = (f32[512,512]{1,0:T(8,128)}, bf16[512,512]{1,0:T(8,128)(2,1)}) custom-call(bf16[512,256]{1,0:T(8,128)(2,1)} %query_ref.1, bf16[512,256]{1,0:T(8,128)(2,1)} %key_ref.3, f32[512,4]{1,0:T(8,128)} %get-tuple-element.24.cum_ref, bf16[8,256,128]{2,1,0:T(8,128)(2,1)} %get-tuple-element.25.inner_ref, ...), custom_call_target="tpu_custom_call" | custom-call | flops 2000000000 | bytes 8000000 | tf_op jit(solution)/shard_map/block_reads/pallas_call | solution.py:214
  28.2 5.1 %all-to-all-done.maps_ref = bf16[8,192,128]{2,1,0:T(8,128)(2,1)S(1)} async-done(((bf16[8,192,128]{2,1,0:T(8,128)(2,1)}), bf16[8,192,128]{2,1,0:T(8,128)(2,1)S(1)}, u32[]{:S(2)}, u32[]{:S(2)}) %all-to-all-start) | async-done | bytes 393248 | tf_op jit(solution)/shard_map/all_to_all | solution.py:478
  33.3 1.0 row_total.1
  35.0 4.8 %all-to-all-start.1 = ((bf16[4,192,128]{2,1,0:T(8,128)(2,1)}), bf16[4,192,128]{2,1,0:T(8,128)(2,1)S(1)}, u32[]{:S(2)}, u32[]{:S(2)}) async-start(bf16[4,192,128]{2,1,0:T(8,128)(2,1)} %copy-done.2), calls=%async_computation.1 | async-start | bytes 393216 | tf_op jit(solution)/shard_map/all_to_all | solution.py:486
  39.9 4.9 %all-to-all-done.1.totals_ref = bf16[4,192,128]{2,1,0:T(8,128)(2,1)S(1)} async-done(((bf16[4,192,128]{2,1,0:T(8,128)(2,1)}), bf16[4,192,128]{2,1,0:T(8,128)(2,1)S(1)}, u32[]{:S(2)}, u32[]{:S(2)}) %all-to-all-start.1) | async-done | bytes 196640 | tf_op jit(solution)/shard_map/all_to_all | solution.py:486
  44.7 1.3 shard_starts.1
  46.0 12.1 %all_to_all.40 = bf16[8,64,128]{2,1,0:T(8,128)(2,1)} all-to-all(bf16[8,64,128]{2,1,0:T(8,128)(2,1)S(1)} %shard_starts.1), channel_id=1, replica_groups={{0,8,16,24,32,40,48,56},{64,72,80,88,96,104,112,120},{128,136,144,152,1..., dimensions={0} | all-to-all | bytes 262144 | tf_op jit(solution)/shard_map/all_to_all | solution.py:478
  58.1 4.8 %gated_part.1 = (bf16[256,512]{1,0:T(8,128)(2,1)}, bf16[256,2048]{1,0:T(8,128)(2,1)}) custom-call(s32[1]{0:T(128)} %bitcast.core_side, f32[512,512]{1,0:T(8,128)} %get-tuple-element.32.core_ref, bf16[512,512]{1,0:T(8,128)(2,1)} %get-tuple-element.33.reach_ref, bf16[512,128]{1,0:T(8,128)(2,1)} %bitcast.38, bf16[512,512]{1,0:T(8,128)(2,1)} %gate_ref.1, ...), custom_call_target="tpu_custom_call" | custom-call | tf_op jit(solution)/shard_map/gated_part/pallas_call | solution.py:304
  63.3 1.6 copy-done.1
  64.9 0.9 copy-done.6
  67.0 20.0 %all_to_all.41.parts_ref = bf16[4,64,2048]{2,1,0:T(8,128)(2,1)S(1)} all-to-all(bf16[4,64,2048]{2,1,0:T(8,128)(2,1)S(1)} %bitcast.34), channel_id=1, replica_groups={{0,2,4,6},{1,3,5,7},{8,10,12,14},{9,11,13,15},{16,18,20,22},{17,19,21,2..., dimensions={0} | all-to-all | bytes 2097152 | tf_op jit(solution)/shard_map/all_to_all | solution.py:470
  87.3 17.4 %all_to_all.42 = bf16[4,64,2048]{2,1,0:T(8,128)(2,1)S(1)} all-to-all(bf16[4,64,2048]{2,1,0:T(8,128)(2,1)S(1)} %get-tuple-element.40), channel_id=1, replica_groups={{0,2,4,6},{1,3,5,7},{8,10,12,14},{9,11,13,15},{16,18,20,22},{17,19,21,2..., dimensions={0} | all-to-all | bytes 2097152 | tf_op jit(solution)/shard_map/all_to_all | solution.py:470
  104.7 2.7 collective-permute-done.1.other_ref
  107.4 2.3 pick_rows.1
  109.7 76.1 %all_to_all.43 = bf16[32,24,2048]{2,1,0:T(8,128)(2,1)S(1)} all-to-all(bf16[32,24,2048]{2,1,0:T(8,128)(2,1)S(1)} %bitcast.30), channel_id=1, replica_groups=mesh['node'=32,'local'=8] {'node'}, dimensions={0} | all-to-all | bytes 6291456 | tf_op jit(solution)/shard_map/all_to_all | solution.py:492
  185.7 3.4 %fusion = f32[768,1024]{1,0:T(8,128)S(1)} fusion(bf16[768,2048]{1,0:T(8,128)(2,1)S(1)} %bitcast.36, bf16[1,2048,1024]{2,1,0:T(8,128)(2,1)S(1)} %copy-done.8), kind=kOutput, calls=%fused_computation | convolution fusion | flops 3221225472 | bytes 10485760 | tf_op jit(solution)/shard_map/dot_general | solution.py:537
  189.2 1.8 convolution_convert_fusion
  191.0 78.4 %all_to_all.44 = bf16[32,24,2048]{2,1,0:T(8,128)(2,1)S(1)} all-to-all(bf16[32,24,2048]{2,1,0:T(8,128)(2,1)S(1)} %bitcast.37), channel_id=1, replica_groups=mesh['node'=32,'local'=8] {'node'}, dimensions={0} | all-to-all | bytes 6291456 | tf_op jit(solution)/shard_map/all_to_all | solution.py:492
  269.4 1.0 merge_rows.3
  270.5 1.0 merge_rows.2
  271.5 1.7 collective-permute-done.2
  273.6 18.1 %all_to_all.45 = bf16[4,64,2048]{2,1,0:T(8,128)(2,1)S(1)} all-to-all(bf16[4,64,2048]{2,1,0:T(8,128)(2,1)S(1)} %bitcast.35), channel_id=1, replica_groups={{0,2,4,6},{1,3,5,7},{8,10,12,14},{9,11,13,15},{16,18,20,22},{17,19,21,2..., dimensions={0} | all-to-all | bytes 2097152 | tf_op jit(solution)/shard_map/all_to_all | solution.py:470
  (35 shorter events, 7.2 us)
Async XLA Ops:
  0.0 189.2 %copy-start = (bf16[1,512,2048]{2,1,0:T(8,128)(2,1)S(1)}, bf16[1,512,2048]{2,1,0:T(8,128)(2,1)}, u32[]{:S(2)}) copy-start(bf16[1,512,2048]{2,1,0:T(8,128)(2,1)} %param.27) | copy-start | bytes 6291460
  10.1 23.2 %all-to-all-start = ((bf16[8,192,128]{2,1,0:T(8,128)(2,1)}), bf16[8,192,128]{2,1,0:T(8,128)(2,1)S(1)}, u32[]{:S(2)}, u32[]{:S(2)}) async-start(bf16[8,192,128]{2,1,0:T(8,128)(2,1)} %get-tuple-element.23), calls=%async_computation | async-start | bytes 786432 | tf_op jit(solution)/shard_map/all_to_all | solution.py:478
  27.3 0.9 copy-start.3
  34.4 0.7 copy-start.2
  35.0 9.7 %all-to-all-start.1 = ((bf16[4,192,128]{2,1,0:T(8,128)(2,1)}), bf16[4,192,128]{2,1,0:T(8,128)(2,1)S(1)}, u32[]{:S(2)}, u32[]{:S(2)}) async-start(bf16[4,192,128]{2,1,0:T(8,128)(2,1)} %copy-done.2), calls=%async_computation.1 | async-start | bytes 393216 | tf_op jit(solution)/shard_map/all_to_all | solution.py:486
  63.0 3.6 %collective-permute-start = (bf16[256,2048]{1,0:T(8,128)(2,1)}, bf16[256,2048]{1,0:T(8,128)(2,1)S(1)}, u32[]{:S(2)}, u32[]{:S(2)}) collective-permute-start(bf16[256,2048]{1,0:T(8,128)(2,1)} %get-tuple-element.36), channel_id=1, source_target_pairs={{0,1},{1,0},{2,3},{3,2},{4,5},{5,4},{6,7},{7,6},{8,9},{9,8},{10,11... | collective-permute-start | bytes 3145736 | tf_op jit(solution)/shard_map/ppermute | solution.py:465
  63.3 1.6 copy-start.1
  64.9 0.9 copy-start.6
  66.5 20.5 %copy-start.5 = (bf16[64,2048]{1,0:T(8,128)(2,1)S(1)}, bf16[64,2048]{1,0:T(8,128)(2,1)}, u32[]{:S(2)}) copy-start(bf16[64,2048]{1,0:T(8,128)(2,1)} %hidden_ref.1) | copy-start | bytes 786436
  66.5 20.5 %copy-start.7 = (f32[2048]{0:T(1024)S(1)}, f32[2048]{0:T(1024)}, u32[]{:S(2)}) copy-start(f32[2048]{0:T(1024)} %param.23) | copy-start | bytes 24580
  87.0 20.3 %copy-start.4 = (bf16[768,512]{1,0:T(8,128)(2,1)S(1)}, bf16[768,512]{1,0:T(8,128)(2,1)}, u32[]{:S(2)}) copy-start(bf16[768,512]{1,0:T(8,128)(2,1)} %copy-done.3) | copy-start | bytes 2359300
  104.7 2.7 collective-permute-start.1
  109.7 76.1 %copy-start.8 = (bf16[1,2048,1024]{2,1,0:T(8,128)(2,1)S(1)}, bf16[1,2048,1024]{2,1,0:T(8,128)(2,1)}, u32[]{:S(2)}) copy-start(bf16[1,2048,1024]{2,1,0:T(8,128)(2,1)} %param.26) | copy-start | bytes 12582916
  270.4 2.7 collective-permute-start.2

commit v5 on v4

--- a/solution.py
+++ b/solution.py
@@ -416,25 +416,35 @@
     )(place, index, weight)
 
 
-def pick_kernel(pick_ref, own_ref, other_ref, out_ref):
-    half = own_ref.shape[0]
-    out_ref[...] = (mm(pick_ref[:, :half], own_ref[...]) + mm(pick_ref[:, half:], other_ref[...])).astype(bf16)
-
-
-def pick_rows(pick, own, other):
-    slots, tokens = pick.shape
-    half, width = own.shape
-    tile = 1024
-    half_spec = pl.BlockSpec((half, tile), lambda i: (0, i))
-    return pl.pallas_call(
-        pick_kernel,
+def pick_kernel(pick_ref, rows_ref, out_ref):
+    out_ref[...] = mm(pick_ref[...], rows_ref[...]).astype(bf16)
+
+
+def pick_more_kernel(pick_ref, rows_ref, found_ref, out_ref):
+    out_ref[...] = (mm(pick_ref[...], rows_ref[...]) + found_ref[...].astype(f32)).astype(bf16)
+
+
+def pick_rows(pick, half, rows, *found):
+    slots = pick.shape[0]
+    tokens, width = rows.shape
+    tile = width // 2
+    out_spec = pl.BlockSpec((slots, tile), lambda i: (0, i))
+    return pl.pallas_call(
+        pick_more_kernel if found else pick_kernel,
         out_shape=jax.ShapeDtypeStruct((slots, width), bf16),
         grid=(width // tile,),
-        in_specs=[pl.BlockSpec((slots, tokens), lambda i: (0, 0)), half_spec, half_spec],
-        out_specs=pl.BlockSpec((slots, tile), lambda i: (0, i)),
-        compiler_params=pltpu.CompilerParams(vmem_limit_bytes=32 * 2**20),
+        in_specs=[
+            pl.BlockSpec((slots, tokens), lambda i: (0, half)),
+            pl.BlockSpec((tokens, tile), lambda i: (0, i)),
+        ]
+        + [out_spec] * len(found),
+        out_specs=out_spec,
+        compiler_params=pltpu.CompilerParams(vmem_limit_bytes=32 * 2**20),
+        cost_estimate=pl.CostEstimate(
+            flops=2 * slots * tokens * width, bytes_accessed=5 * 10**6, transcendentals=0
+        ),
         name="pick_rows",
-    )(pick, own, other)
+    )(pick, rows, *found)
 
 
 def merge_kernel(merge_ref, rows_ref, out_ref):
@@ -532,7 +542,9 @@
     parts = across_chips(partial.reshape(chips, share, width))
     hidden_state, normed = residual(parts, hidden_in, post_gain.reshape(1, width))
     own_rows = across_chips(normed).reshape(chips * share, width)
-    rows = pick_rows(pick, own_rows, swap_cores(own_rows)).reshape(node_count, capacity, width)
+    other_rows = swap_cores(own_rows)
+    found = pick_rows(pick, 0, own_rows)
+    rows = pick_rows(pick, 1, other_rows, found).reshape(node_count, capacity, width)
     rows = across_nodes(rows).reshape(node_count * capacity, width)
     gate_up = jnp.dot(rows, expert_gate_up[0], preferred_element_type=f32)
     half_width = gate_up.shape[1] // 2

time: 296 us -> 295 us (level)
  no operation moved by 1% of the time
where the time goes in v5:
time: 295 us; the launch traced here: 292 us
  blocking collectives  222 us (75%)
  Pallas kernels  30.2 us (10%)
  starting transfers between devices  13.7 us (5%)
  waiting for transfers between devices  12.8 us (4%)
  local copies, waits for them, and re-layouts  6.04 us (2%)
  matrix products  5.27 us (2%)
    all_to_all x2, blocking collectives, across_nodes(): lax.all_to_all(array, 'node', split_axis=0, concat_axis=0, tiled=True)  154 us
    all_to_all x3, blocking collectives, across_chips(): lax.all_to_all(array, 'local', split_axis=0, concat_axis=0, tiled=True, a...  55.5 us
    all_to_all x1, blocking collectives, along_row(): lax.all_to_all(array, 'node', split_axis=0, concat_axis=0, tiled=True, ax...  12.1 us
    pallas_call x1, Pallas kernels, shard_maps(): pl.pallas_call(maps_kernel, out_shape=(jax.ShapeDtypeStruct((HEADS * SPLI...  10.1 us
    all_to_all x1, starting transfers between devices, along_row(): lax.all_to_all(array, 'node', split_axis=0, concat_axis=0, tiled=True, ax...  8.47 us
    pallas_call x1, Pallas kernels, block_reads(): pl.pallas_call(reads_kernel, out_shape=(jax.ShapeDtypeStruct((tokens, HEA...  6.12 us
  transfers between devices with their start and end apart: 5, of which 4 were waited for; matrix products, arithmetic and copies ran while one was open for 1% of the time, Pallas kernels for 3%

profile of v5, /device:TPU:2, one launch (start us, length us, event | category | flops | bytes accessed | tf_op | source)
XLA Modules:
  0.0 292.0 jit_solution(3151125718857892711)
XLA Ops:
  0.0 10.1 %shard_maps.1 = (bf16[8,192,128]{2,1,0:T(8,128)(2,1)}, f32[512,4]{1,0:T(8,128)}, bf16[8,256,128]{2,1,0:T(8,128)(2,1)}, bf16[8,256,128]{2,1,0:T(8,128)(2,1)}, bf16[8,4,128,256]{3,2,1,0:T(8,128)(2,1)}) custom-call(bf16[512,256]{1,0:T(8,128)(2,1)} %key_ref.3, bf16[512,512]{1,0:T(8,128)(2,1)} %value_ref.1, f32[4,512]{1,0:T(4,128)} %bitcast.41, f32[4,512]{1,0:T(4,128)} %bitcast.42), custom_call_target="tpu_custom_call" | custom-call | tf_op jit(solution)/shard_map/shard_maps/pallas_call | solution.py:166
  10.1 8.5 %all-to-all-start = ((bf16[8,192,128]{2,1,0:T(8,128)(2,1)}), bf16[8,192,128]{2,1,0:T(8,128)(2,1)S(1)}, u32[]{:S(2)}, u32[]{:S(2)}) async-start(bf16[8,192,128]{2,1,0:T(8,128)(2,1)} %get-tuple-element.23), calls=%async_computation | async-start | bytes 786432 | tf_op jit(solution)/shard_map/all_to_all | solution.py:488
  20.6 6.1 %block_reads.1 = (f32[512,512]{1,0:T(8,128)}, bf16[512,512]{1,0:T(8,128)(2,1)}) custom-call(bf16[512,256]{1,0:T(8,128)(2,1)} %query_ref.1, bf16[512,256]{1,0:T(8,128)(2,1)} %key_ref.3, f32[512,4]{1,0:T(8,128)} %get-tuple-element.24.cum_ref, bf16[8,256,128]{2,1,0:T(8,128)(2,1)} %get-tuple-element.25.inner_ref, ...), custom_call_target="tpu_custom_call" | custom-call | flops 2000000000 | bytes 8000000 | tf_op jit(solution)/shard_map/block_reads/pallas_call | solution.py:214
  28.2 5.1 %all-to-all-done.maps_ref = bf16[8,192,128]{2,1,0:T(8,128)(2,1)S(1)} async-done(((bf16[8,192,128]{2,1,0:T(8,128)(2,1)}), bf16[8,192,128]{2,1,0:T(8,128)(2,1)S(1)}, u32[]{:S(2)}, u32[]{:S(2)}) %all-to-all-start) | async-done | bytes 393248 | tf_op jit(solution)/shard_map/all_to_all | solution.py:488
  33.3 1.0 row_total.1
  35.0 4.8 %all-to-all-start.1 = ((bf16[4,192,128]{2,1,0:T(8,128)(2,1)}), bf16[4,192,128]{2,1,0:T(8,128)(2,1)S(1)}, u32[]{:S(2)}, u32[]{:S(2)}) async-start(bf16[4,192,128]{2,1,0:T(8,128)(2,1)} %copy-done.4), calls=%async_computation.1 | async-start | bytes 393216 | tf_op jit(solution)/shard_map/all_to_all | solution.py:496
  39.9 4.9 %all-to-all-done.1.totals_ref = bf16[4,192,128]{2,1,0:T(8,128)(2,1)S(1)} async-done(((bf16[4,192,128]{2,1,0:T(8,128)(2,1)}), bf16[4,192,128]{2,1,0:T(8,128)(2,1)S(1)}, u32[]{:S(2)}, u32[]{:S(2)}) %all-to-all-start.1) | async-done | bytes 196640 | tf_op jit(solution)/shard_map/all_to_all | solution.py:496
  44.7 1.3 shard_starts.1
  46.0 12.1 %all_to_all.40 = bf16[8,64,128]{2,1,0:T(8,128)(2,1)} all-to-all(bf16[8,64,128]{2,1,0:T(8,128)(2,1)S(1)} %shard_starts.1), channel_id=1, replica_groups={{0,8,16,24,32,40,48,56},{64,72,80,88,96,104,112,120},{128,136,144,152,1..., dimensions={0} | all-to-all | bytes 262144 | tf_op jit(solution)/shard_map/all_to_all | solution.py:488
  58.1 4.8 %gated_part.1 = (bf16[256,512]{1,0:T(8,128)(2,1)}, bf16[256,2048]{1,0:T(8,128)(2,1)}) custom-call(s32[1]{0:T(128)} %bitcast.core_side, f32[512,512]{1,0:T(8,128)} %get-tuple-element.32.core_ref, bf16[512,512]{1,0:T(8,128)(2,1)} %get-tuple-element.33.reach_ref, bf16[512,128]{1,0:T(8,128)(2,1)} %bitcast.38, bf16[512,512]{1,0:T(8,128)(2,1)} %gate_ref.1, ...), custom_call_target="tpu_custom_call" | custom-call | tf_op jit(solution)/shard_map/gated_part/pallas_call | solution.py:304
  63.3 1.6 copy-done.1
  67.0 20.0 %all_to_all.41.parts_ref = bf16[4,64,2048]{2,1,0:T(8,128)(2,1)S(1)} all-to-all(bf16[4,64,2048]{2,1,0:T(8,128)(2,1)S(1)} %bitcast.34), channel_id=1, replica_groups={{0,2,4,6},{1,3,5,7},{8,10,12,14},{9,11,13,15},{16,18,20,22},{17,19,21,2..., dimensions={0} | all-to-all | bytes 2097152 | tf_op jit(solution)/shard_map/all_to_all | solution.py:480
  87.3 17.4 %all_to_all.42 = bf16[4,64,2048]{2,1,0:T(8,128)(2,1)S(1)} all-to-all(bf16[4,64,2048]{2,1,0:T(8,128)(2,1)S(1)} %get-tuple-element.40), channel_id=1, replica_groups={{0,2,4,6},{1,3,5,7},{8,10,12,14},{9,11,13,15},{16,18,20,22},{17,19,21,2..., dimensions={0} | all-to-all | bytes 2097152 | tf_op jit(solution)/shard_map/all_to_all | solution.py:480
  104.7 1.5 pick_rows.2.found_ref
  106.2 1.2 collective-permute-done.1.rows_ref
  107.3 1.7 pick_rows.3
  109.1 76.1 %all_to_all.43 = bf16[32,24,2048]{2,1,0:T(8,128)(2,1)S(1)} all-to-all(bf16[32,24,2048]{2,1,0:T(8,128)(2,1)S(1)} %bitcast.30), channel_id=1, replica_groups=mesh['node'=32,'local'=8] {'node'}, dimensions={0} | all-to-all | bytes 6291456 | tf_op jit(solution)/shard_map/all_to_all | solution.py:502
  185.1 3.4 %fusion = f32[768,1024]{1,0:T(8,128)S(1)} fusion(bf16[768,2048]{1,0:T(8,128)(2,1)S(1)} %bitcast.36, bf16[1,2048,1024]{2,1,0:T(8,128)(2,1)S(1)} %copy-done.8), kind=kOutput, calls=%fused_computation | convolution fusion | flops 3221225472 | bytes 10485760 | tf_op jit(solution)/shard_map/dot_general | solution.py:549
  188.6 1.8 convolution_convert_fusion
  190.4 78.4 %all_to_all.44 = bf16[32,24,2048]{2,1,0:T(8,128)(2,1)S(1)} all-to-all(bf16[32,24,2048]{2,1,0:T(8,128)(2,1)S(1)} %bitcast.37), channel_id=1, replica_groups=mesh['node'=32,'local'=8] {'node'}, dimensions={0} | all-to-all | bytes 6291456 | tf_op jit(solution)/shard_map/all_to_all | solution.py:502
  268.8 1.0 merge_rows.3
  269.9 1.0 merge_rows.2
  270.9 1.7 collective-permute-done.2
  273.0 18.1 %all_to_all.45 = bf16[4,64,2048]{2,1,0:T(8,128)(2,1)S(1)} all-to-all(bf16[4,64,2048]{2,1,0:T(8,128)(2,1)S(1)} %bitcast.35), channel_id=1, replica_groups={{0,2,4,6},{1,3,5,7},{8,10,12,14},{9,11,13,15},{16,18,20,22},{17,19,21,2..., dimensions={0} | all-to-all | bytes 2097152 | tf_op jit(solution)/shard_map/all_to_all | solution.py:480
  (36 shorter events, 8.2 us)
Async XLA Ops:
  0.0 188.6 %copy-start = (bf16[1,512,2048]{2,1,0:T(8,128)(2,1)S(1)}, bf16[1,512,2048]{2,1,0:T(8,128)(2,1)}, u32[]{:S(2)}) copy-start(bf16[1,512,2048]{2,1,0:T(8,128)(2,1)} %param.27) | copy-start | bytes 6291460
  10.1 23.2 %all-to-all-start = ((bf16[8,192,128]{2,1,0:T(8,128)(2,1)}), bf16[8,192,128]{2,1,0:T(8,128)(2,1)S(1)}, u32[]{:S(2)}, u32[]{:S(2)}) async-start(bf16[8,192,128]{2,1,0:T(8,128)(2,1)} %get-tuple-element.23), calls=%async_computation | async-start | bytes 786432 | tf_op jit(solution)/shard_map/all_to_all | solution.py:488
  27.3 0.9 copy-start.2
  34.4 0.7 copy-start.4
  35.0 9.7 %all-to-all-start.1 = ((bf16[4,192,128]{2,1,0:T(8,128)(2,1)}), bf16[4,192,128]{2,1,0:T(8,128)(2,1)S(1)}, u32[]{:S(2)}, u32[]{:S(2)}) async-start(bf16[4,192,128]{2,1,0:T(8,128)(2,1)} %copy-done.4), calls=%async_computation.1 | async-start | bytes 393216 | tf_op jit(solution)/shard_map/all_to_all | solution.py:496
  63.0 3.6 %collective-permute-start = (bf16[256,2048]{1,0:T(8,128)(2,1)}, bf16[256,2048]{1,0:T(8,128)(2,1)S(1)}, u32[]{:S(2)}, u32[]{:S(2)}) collective-permute-start(bf16[256,2048]{1,0:T(8,128)(2,1)} %get-tuple-element.36), channel_id=1, source_target_pairs={{0,1},{1,0},{2,3},{3,2},{4,5},{5,4},{6,7},{7,6},{8,9},{9,8},{10,11... | collective-permute-start | bytes 3145736 | tf_op jit(solution)/shard_map/ppermute | solution.py:475
  63.3 1.6 copy-start.1
  64.9 0.9 copy-start.6
  66.5 20.5 %copy-start.5 = (bf16[64,2048]{1,0:T(8,128)(2,1)S(1)}, bf16[64,2048]{1,0:T(8,128)(2,1)}, u32[]{:S(2)}) copy-start(bf16[64,2048]{1,0:T(8,128)(2,1)} %hidden_ref.1) | copy-start | bytes 786436
  66.5 20.5 %copy-start.7 = (f32[2048]{0:T(1024)S(1)}, f32[2048]{0:T(1024)}, u32[]{:S(2)}) copy-start(f32[2048]{0:T(1024)} %param.23) | copy-start | bytes 24580
  87.0 17.7 %copy-start.3 = (bf16[768,512]{1,0:T(8,128)(2,1)S(1)}, bf16[768,512]{1,0:T(8,128)(2,1)}, u32[]{:S(2)}) copy-start(bf16[768,512]{1,0:T(8,128)(2,1)} %copy-done.2) | copy-start | bytes 2359300
  104.7 2.7 collective-permute-start.1
  109.1 76.1 %copy-start.8 = (bf16[1,2048,1024]{2,1,0:T(8,128)(2,1)S(1)}, bf16[1,2048,1024]{2,1,0:T(8,128)(2,1)}, u32[]{:S(2)}) copy-start(bf16[1,2048,1024]{2,1,0:T(8,128)(2,1)} %param.26) | copy-start | bytes 12582916
  269.8 2.7 collective-permute-start.2

commit v6 on v5

--- a/solution.py
+++ b/solution.py
@@ -322,11 +322,11 @@
     )(side, core, reach, starts, gate, gain, weight)
 
 
-def project_kernel(rows_ref, weight_ref, out_ref):
-    out_ref[...] = mm(rows_ref[...], weight_ref[...]).astype(bf16)
-
-
-def project(rows, weight):
+def project_kernel(rows_ref, weight_ref, given_ref, out_ref):
+    out_ref[...] = (mm(rows_ref[...], weight_ref[...]) + given_ref[...].astype(f32)).astype(bf16)
+
+
+def project(rows, weight, given):
     return pl.pallas_call(
         project_kernel,
         out_shape=jax.ShapeDtypeStruct((rows.shape[0], weight.shape[1]), bf16),
@@ -335,7 +335,7 @@
             flops=2 * rows.size * weight.shape[1], bytes_accessed=4 * 10**6, transcendentals=0
         ),
         name="project",
-    )(rows, weight)
+    )(rows, weight, given)
 
 
 def residual_kernel(parts_ref, hidden_ref, gain_ref, state_ref, normed_ref):
@@ -358,6 +358,22 @@
         compiler_params=pltpu.CompilerParams(vmem_limit_bytes=32 * 2**20),
         name="residual",
     )(parts, hidden, gain)
+
+
+def finish_kernel(parts_ref, state_ref, out_ref):
+    total = state_ref[...]
+    for part in range(parts_ref.shape[0]):
+        total = total + parts_ref[part].astype(f32)
+    out_ref[...] = total.astype(bf16)
+
+
+def finish(parts, state):
+    return pl.pallas_call(
+        finish_kernel,
+        out_shape=jax.ShapeDtypeStruct(state.shape, bf16),
+        compiler_params=pltpu.CompilerParams(vmem_limit_bytes=32 * 2**20),
+        name="finish",
+    )(parts, state)
 
 
 def routing_kernel(capacity, place_ref, index_ref, weight_ref, pick_ref, merge_ref, slot_s, share_s, wide_s):
@@ -536,9 +552,7 @@
     own_half, other_part = gated_part(
         side_array, core, reach, carried, out_gate, norm_gain.reshape(1, DV), out_weight
     )
-    given_part = swap_cores(other_part)
-    kept_part = project(own_half, out_weight)
-    partial = (kept_part.astype(f32) + given_part.astype(f32)).astype(bf16)
+    partial = project(own_half, out_weight, swap_cores(other_part))
     parts = across_chips(partial.reshape(chips, share, width))
     hidden_state, normed = residual(parts, hidden_in, post_gain.reshape(1, width))
     own_rows = across_chips(normed).reshape(chips * share, width)
@@ -557,7 +571,7 @@
     kept = merge_rows(merge, 0, returned)
     summed = (kept.astype(f32) + given.astype(f32)).astype(bf16)
     arrived = across_chips(summed.reshape(chips, share, width))
-    return (hidden_state + jnp.sum(arrived.astype(f32), axis=0)).astype(bf16)
+    return finish(arrived, hidden_state)
 
 
 def solution(mesh):

time: 295 us -> 297 us (level)
  transfers between devices with their start and end apart: 5 -> 5, of which waited for: 4 -> 5; matrix products, arithmetic and copies ran while one was open for 1% -> 1% of each run, Pallas kernels for 3% -> 3%
where the time goes in v6:
time: 297 us; the launch traced here: 293 us
  blocking collectives  221 us (74%)
  Pallas kernels  31 us (10%)
  waiting for transfers between devices  15.7 us (5%)
  starting transfers between devices  13.7 us (5%)
  local copies, waits for them, and re-layouts  6.01 us (2%)
  matrix products  5.27 us (2%)
    all_to_all x2, blocking collectives, across_nodes(): lax.all_to_all(array, 'node', split_axis=0, concat_axis=0, tiled=True)  154 us
    all_to_all x3, blocking collectives, across_chips(): lax.all_to_all(array, 'local', split_axis=0, concat_axis=0, tiled=True, a...  54.5 us
    all_to_all x1, blocking collectives, along_row(): lax.all_to_all(array, 'node', split_axis=0, concat_axis=0, tiled=True, ax...  12.1 us
    pallas_call x1, Pallas kernels, shard_maps(): pl.pallas_call(maps_kernel, out_shape=(jax.ShapeDtypeStruct((HEADS * SPLI...  10.1 us
    all_to_all x1, starting transfers between devices, along_row(): lax.all_to_all(array, 'node', split_axis=0, concat_axis=0, tiled=True, ax...  8.47 us
    pallas_call x1, Pallas kernels, block_reads(): pl.pallas_call(reads_kernel, out_shape=(jax.ShapeDtypeStruct((tokens, HEA...  6.11 us
  transfers between devices with their start and end apart: 5, of which 5 were waited for; matrix products, arithmetic and copies ran while one was open for 1% of the time, Pallas kernels for 3%

profile of v6, /device:TPU:2, one launch (start us, length us, event | category | flops | bytes accessed | tf_op | source)
XLA Modules:
  0.0 293.4 jit_solution(8474621674890873800)
XLA Ops:
  0.0 10.1 %shard_maps.1 = (bf16[8,192,128]{2,1,0:T(8,128)(2,1)}, f32[512,4]{1,0:T(8,128)}, bf16[8,256,128]{2,1,0:T(8,128)(2,1)}, bf16[8,256,128]{2,1,0:T(8,128)(2,1)}, bf16[8,4,128,256]{3,2,1,0:T(8,128)(2,1)}) custom-call(bf16[512,256]{1,0:T(8,128)(2,1)} %key_ref.3, bf16[512,512]{1,0:T(8,128)(2,1)} %value_ref.1, f32[4,512]{1,0:T(4,128)} %bitcast.41, f32[4,512]{1,0:T(4,128)} %bitcast.42), custom_call_target="tpu_custom_call" | custom-call | tf_op jit(solution)/shard_map/shard_maps/pallas_call | solution.py:166
  10.1 8.5 %all-to-all-start = ((bf16[8,192,128]{2,1,0:T(8,128)(2,1)}), bf16[8,192,128]{2,1,0:T(8,128)(2,1)S(1)}, u32[]{:S(2)}, u32[]{:S(2)}) async-start(bf16[8,192,128]{2,1,0:T(8,128)(2,1)} %get-tuple-element.23), calls=%async_computation | async-start | bytes 786432 | tf_op jit(solution)/shard_map/all_to_all | solution.py:504
  20.6 6.1 %block_reads.1 = (f32[512,512]{1,0:T(8,128)}, bf16[512,512]{1,0:T(8,128)(2,1)}) custom-call(bf16[512,256]{1,0:T(8,128)(2,1)} %query_ref.1, bf16[512,256]{1,0:T(8,128)(2,1)} %key_ref.3, f32[512,4]{1,0:T(8,128)} %get-tuple-element.24.cum_ref, bf16[8,256,128]{2,1,0:T(8,128)(2,1)} %get-tuple-element.25.inner_ref, ...), custom_call_target="tpu_custom_call" | custom-call | flops 2000000000 | bytes 8000000 | tf_op jit(solution)/shard_map/block_reads/pallas_call | solution.py:214
  28.2 5.1 %all-to-all-done.maps_ref = bf16[8,192,128]{2,1,0:T(8,128)(2,1)S(1)} async-done(((bf16[8,192,128]{2,1,0:T(8,128)(2,1)}), bf16[8,192,128]{2,1,0:T(8,128)(2,1)S(1)}, u32[]{:S(2)}, u32[]{:S(2)}) %all-to-all-start) | async-done | bytes 393248 | tf_op jit(solution)/shard_map/all_to_all | solution.py:504
  33.3 1.0 row_total.1
  35.0 4.8 %all-to-all-start.1 = ((bf16[4,192,128]{2,1,0:T(8,128)(2,1)}), bf16[4,192,128]{2,1,0:T(8,128)(2,1)S(1)}, u32[]{:S(2)}, u32[]{:S(2)}) async-start(bf16[4,192,128]{2,1,0:T(8,128)(2,1)} %copy-done.4), calls=%async_computation.1 | async-start | bytes 393216 | tf_op jit(solution)/shard_map/all_to_all | solution.py:512
  39.9 4.9 %all-to-all-done.1.totals_ref = bf16[4,192,128]{2,1,0:T(8,128)(2,1)S(1)} async-done(((bf16[4,192,128]{2,1,0:T(8,128)(2,1)}), bf16[4,192,128]{2,1,0:T(8,128)(2,1)S(1)}, u32[]{:S(2)}, u32[]{:S(2)}) %all-to-all-start.1) | async-done | bytes 196640 | tf_op jit(solution)/shard_map/all_to_all | solution.py:512
  44.7 1.3 shard_starts.1
  46.0 12.1 %all_to_all.40 = bf16[8,64,128]{2,1,0:T(8,128)(2,1)} all-to-all(bf16[8,64,128]{2,1,0:T(8,128)(2,1)S(1)} %shard_starts.1), channel_id=1, replica_groups={{0,8,16,24,32,40,48,56},{64,72,80,88,96,104,112,120},{128,136,144,152,1..., dimensions={0} | all-to-all | bytes 262144 | tf_op jit(solution)/shard_map/all_to_all | solution.py:504
  58.1 4.9 %gated_part.1 = (bf16[256,512]{1,0:T(8,128)(2,1)}, bf16[256,2048]{1,0:T(8,128)(2,1)}) custom-call(s32[1]{0:T(128)} %bitcast.7.core_side, f32[512,512]{1,0:T(8,128)} %get-tuple-element.34.core_ref, bf16[512,512]{1,0:T(8,128)(2,1)} %get-tuple-element.35.reach_ref, bf16[512,128]{1,0:T(8,128)(2,1)} %bitcast.38, bf16[512,512]{1,0:T(8,128)(2,1)} %gate_ref.1, ...), custom_call_target="tpu_custom_call" | custom-call | tf_op jit(solution)/shard_map/gated_part/pallas_call | solution.py:304
  63.3 2.9 collective-permute-done.given_ref
  66.1 1.6 copy-done.1
  69.4 19.8 %all_to_all.41.parts_ref = bf16[4,64,2048]{2,1,0:T(8,128)(2,1)S(1)} all-to-all(bf16[4,64,2048]{2,1,0:T(8,128)(2,1)S(1)} %bitcast.33), channel_id=1, replica_groups={{0,2,4,6},{1,3,5,7},{8,10,12,14},{9,11,13,15},{16,18,20,22},{17,19,21,2..., dimensions={0} | all-to-all | bytes 2097152 | tf_op jit(solution)/shard_map/all_to_all | solution.py:496
  89.5 16.7 %all_to_all.42 = bf16[4,64,2048]{2,1,0:T(8,128)(2,1)S(1)} all-to-all(bf16[4,64,2048]{2,1,0:T(8,128)(2,1)S(1)} %get-tuple-element.39), channel_id=1, replica_groups={{0,2,4,6},{1,3,5,7},{8,10,12,14},{9,11,13,15},{16,18,20,22},{17,19,21,2..., dimensions={0} | all-to-all | bytes 2097152 | tf_op jit(solution)/shard_map/all_to_all | solution.py:496
  106.2 1.5 pick_rows.2.found_ref
  107.7 1.2 collective-permute-done.1.rows_ref
  108.8 1.7 pick_rows.3
  110.6 76.1 %all_to_all.43 = bf16[32,24,2048]{2,1,0:T(8,128)(2,1)S(1)} all-to-all(bf16[32,24,2048]{2,1,0:T(8,128)(2,1)S(1)} %bitcast.30), channel_id=1, replica_groups=mesh['node'=32,'local'=8] {'node'}, dimensions={0} | all-to-all | bytes 6291456 | tf_op jit(solution)/shard_map/all_to_all | solution.py:518
  186.6 3.4 %fusion = f32[768,1024]{1,0:T(8,128)S(1)} fusion(bf16[768,2048]{1,0:T(8,128)(2,1)S(1)} %bitcast.36, bf16[1,2048,1024]{2,1,0:T(8,128)(2,1)S(1)} %copy-done.8), kind=kOutput, calls=%fused_computation | convolution fusion | flops 3221225472 | bytes 10485760 | tf_op jit(solution)/shard_map/dot_general | solution.py:563
  190.1 1.8 convolution_convert_fusion
  191.9 78.4 %all_to_all.44 = bf16[32,24,2048]{2,1,0:T(8,128)(2,1)S(1)} all-to-all(bf16[32,24,2048]{2,1,0:T(8,128)(2,1)S(1)} %bitcast.37), channel_id=1, replica_groups=mesh['node'=32,'local'=8] {'node'}, dimensions={0} | all-to-all | bytes 6291456 | tf_op jit(solution)/shard_map/all_to_all | solution.py:518
  271.4 1.0 merge_rows.2
  272.4 1.7 collective-permute-done.2
  274.5 18.1 %all_to_all.45.parts_ref = bf16[4,64,2048]{2,1,0:T(8,128)(2,1)S(1)} all-to-all(bf16[4,64,2048]{2,1,0:T(8,128)(2,1)S(1)} %bitcast.35), channel_id=1, replica_groups={{0,2,4,6},{1,3,5,7},{8,10,12,14},{9,11,13,15},{16,18,20,22},{17,19,21,2..., dimensions={0} | all-to-all | bytes 2097152 | tf_op jit(solution)/shard_map/all_to_all | solution.py:496
  (34 shorter events, 8.6 us)
Async XLA Ops:
  0.0 190.1 %copy-start = (bf16[1,512,2048]{2,1,0:T(8,128)(2,1)S(1)}, bf16[1,512,2048]{2,1,0:T(8,128)(2,1)}, u32[]{:S(2)}) copy-start(bf16[1,512,2048]{2,1,0:T(8,128)(2,1)} %param.27) | copy-start | bytes 6291460
  10.1 23.2 %all-to-all-start = ((bf16[8,192,128]{2,1,0:T(8,128)(2,1)}), bf16[8,192,128]{2,1,0:T(8,128)(2,1)S(1)}, u32[]{:S(2)}, u32[]{:S(2)}) async-start(bf16[8,192,128]{2,1,0:T(8,128)(2,1)} %get-tuple-element.23), calls=%async_computation | async-start | bytes 786432 | tf_op jit(solution)/shard_map/all_to_all | solution.py:504
  27.3 0.9 copy-start.2
  34.4 0.7 copy-start.4
  35.0 9.7 %all-to-all-start.1 = ((bf16[4,192,128]{2,1,0:T(8,128)(2,1)}), bf16[4,192,128]{2,1,0:T(8,128)(2,1)S(1)}, u32[]{:S(2)}, u32[]{:S(2)}) async-start(bf16[4,192,128]{2,1,0:T(8,128)(2,1)} %copy-done.4), calls=%async_computation.1 | async-start | bytes 393216 | tf_op jit(solution)/shard_map/all_to_all | solution.py:512
  63.0 3.1 %collective-permute-start = (bf16[256,2048]{1,0:T(8,128)(2,1)}, bf16[256,2048]{1,0:T(8,128)(2,1)S(1)}, u32[]{:S(2)}, u32[]{:S(2)}) collective-permute-start(bf16[256,2048]{1,0:T(8,128)(2,1)} %get-tuple-element.38), channel_id=1, source_target_pairs={{0,1},{1,0},{2,3},{3,2},{4,5},{5,4},{6,7},{7,6},{8,9},{9,8},{10,11... | collective-permute-start | bytes 3145736 | tf_op jit(solution)/shard_map/ppermute | solution.py:491
  66.1 1.6 copy-start.1
  67.7 0.9 copy-start.6
  68.7 20.5 %copy-start.5 = (bf16[64,2048]{1,0:T(8,128)(2,1)S(1)}, bf16[64,2048]{1,0:T(8,128)(2,1)}, u32[]{:S(2)}) copy-start(bf16[64,2048]{1,0:T(8,128)(2,1)} %hidden_ref.1) | copy-start | bytes 786436
  68.7 20.5 %copy-start.7 = (f32[2048]{0:T(1024)S(1)}, f32[2048]{0:T(1024)}, u32[]{:S(2)}) copy-start(f32[2048]{0:T(1024)} %param.23) | copy-start | bytes 24580
  69.4 36.8 %copy-start.3 = (bf16[768,512]{1,0:T(8,128)(2,1)S(1)}, bf16[768,512]{1,0:T(8,128)(2,1)}, u32[]{:S(2)}) copy-start(bf16[768,512]{1,0:T(8,128)(2,1)} %copy-done.2) | copy-start | bytes 2359300
  106.2 2.7 collective-permute-start.1
  110.6 76.1 %copy-start.8 = (bf16[1,2048,1024]{2,1,0:T(8,128)(2,1)S(1)}, bf16[1,2048,1024]{2,1,0:T(8,128)(2,1)}, u32[]{:S(2)}) copy-start(bf16[1,2048,1024]{2,1,0:T(8,128)(2,1)} %param.26) | copy-start | bytes 12582916
  271.3 2.7 collective-permute-start.2
